TPU v7x, 32 devices: a whole 2x2x4 slice. The times are simulated.
32 devices in a mesh: section: 2 (over core), wide: 4 (over y, x), rep: 4 (over z).
Axes of the slice: x: 2, y: 2, z: 4, core: 2. Of those that a mesh axis runs over, the one named last changes fastest.
Arguments:
- tokens_in: bfloat16 [2, 4096, 1024], P(None, ('rep', 'wide')), may hold values from -6 to 6
- cotangent: bfloat16 [2, 4096, 1024], P(None, ('rep', 'wide')), may hold values from -6 to 6
- segments: int32 [2, 4096], P(None, 'rep'), may hold values from 0 to 15, never falling along the last dimension, each value on 1 to 1024 neighbouring positions
- routes: int32 [2, 2, 4096, 1], P('section', None, ('rep', 'wide')), may hold values from 0 to 3; in each aligned block of 256 rows (0 to 255, 256 to 511, ..., all dimensions but the last counted through in order) at most 64 rows name the same one
- ln1_gain: float32 [2, 1024], P('section'), may hold values from 0.5 to 1.5
- w_qkv: bfloat16 [2, 1024, 3072], P('section', None, 'wide'), may hold values from -0.1875 to 0.1875
- w_out: bfloat16 [2, 1024, 1024], P('section', 'wide'), may hold values from -2 to 2
- ln2_gain: float32 [2, 1024], P('section'), may hold values from 0.5 to 1.5
- w_up: bfloat16 [2, 1024, 4096], P('section', None, 'wide'), may hold values from -0.1875 to 0.1875
- w_down: bfloat16 [2, 4096, 1024], P('section', 'wide'), may hold values from -0.09375 to 0.09375
- centroids: bfloat16 [2, 4, 1024], P('section', 'wide'), may hold values from -0.125 to 0.125
- sub_gains: float32 [2, 4, 2, 1024], P('section', 'wide'), may hold values from 0.5 to 1.5
- expert_up: bfloat16 [2, 4, 2, 1024, 4096], P('section', 'wide', None, None, 'rep'), may hold values from -0.1875 to 0.1875
- expert_down: bfloat16 [2, 4, 2, 4096, 1024], P('section', 'wide', None, 'rep'), may hold values from -0.09375 to 0.09375
Outputs:
- block_out: bfloat16 [2, 4096, 1024], P(None, ('rep', 'wide'), 'section')
- input_grad: float32 [2, 4096, 1024], P(None, ('rep', 'wide'), 'section')
- grad_ln1: float32 [2, 1024], P('section', ('wide', 'rep'))
- grad_w_qkv: float32 [2, 1024, 3072], P('section', 'rep', 'wide')
- grad_w_out: float32 [2, 1024, 1024], P('section', 'wide', 'rep')
- grad_ln2: float32 [2, 1024], P('section', ('wide', 'rep'))
- grad_w_up: float32 [2, 1024, 4096], P('section', 'rep', 'wide')
- grad_w_down: float32 [2, 4096, 1024], P('section', 'wide', 'rep')
- grad_centroids: float32 [2, 4, 1024], P('section', 'wide', 'rep')
- grad_sub_gains: float32 [2, 4, 2, 1024], P('section', 'wide', None, 'rep')
- grad_expert_up: float32 [2, 4, 2, 1024, 4096], P('section', 'wide', None, None, 'rep')
- grad_expert_down: float32 [2, 4, 2, 4096, 1024], P('section', 'wide', None, 'rep')
Inputs may be any that keep to these rules, and one draw needn't show every extreme that they name: `routes`: among the 256 tokens of one device (aligned blocks of 256 rows of the flattened array), no expert is named more than 64 times, a bound that some block reaches. `segments`: along each micro-batch's tokens the numbers never fall; a document has at most 1024 tokens.
All inputs are finite; a program needn't handle non-finite values.
Results may differ from a plain program's by a relative error of at most 0.025.
Values may be sent and summed in bfloat16 or wider, within the bound.
No kernel may reach another device: no remote copies, remote signals or barrier semaphores. Data moves between devices by JAX's collectives and lax.ppermute only.
A program may use at most 448 MiB of HBM per device.

v0:
```python
import math

import jax
import jax.numpy as jnp
from jax import lax
from jax.sharding import PartitionSpec as P

HD = 64
SEQ_LEN = 1024


epsilon = 1e-05
root_half = 1.0 / math.sqrt(2.0)
root_tau = 1.0 / math.sqrt(2.0 * math.pi)
masked_score = -1e30
highest_prec = lax.Precision.HIGHEST


def partner(value, axis, stride):
    mask = 2**stride
    pairs = [(source, source ^ mask) for source in range(lax.axis_size(axis))]
    return lax.ppermute(value, axis, pairs)


def shortened(value):

    def short(part):
        return part.astype(jnp.bfloat16) if part.dtype == jnp.float32 else part

    return jax.tree.map(short, value)


def matmul(first_arg, second_arg):
    return jnp.dot(first_arg, second_arg, preferred_element_type=jnp.float32)


def matmul_left(first_arg, second_arg):
    return lax.dot_general(
        first_arg, second_arg, (((0,), (0,)), ((), ())), preferred_element_type=jnp.float32
    )


def matmul_right(first_arg, second_arg):
    return lax.dot_general(
        first_arg, second_arg, (((1,), (1,)), ((), ())), preferred_element_type=jnp.float32
    )


def gelu_curve(values):
    return 0.5 * values * (1.0 + lax.erf(values * root_half))


def gelu_slope(values):
    return (
        0.5 * (1.0 + lax.erf(values * root_half))
        + values * jnp.exp(-0.5 * values * values) * root_tau
    )


def norm_forward(values, gain_vec):
    center = values - jnp.mean(values, axis=-1, keepdims=True)
    scale_inv = lax.rsqrt(jnp.mean(center * center, axis=-1, keepdims=True) + epsilon)
    normal = center * scale_inv
    return (normal * gain_vec, normal, scale_inv)


def norm_backward(grad_out, normal, scale_inv, gain_vec):
    scaled = grad_out * gain_vec
    grad_values = scale_inv * (
        scaled
        - jnp.mean(scaled, axis=-1, keepdims=True)
        - normal * jnp.mean(scaled * normal, axis=-1, keepdims=True)
    )
    return (grad_values, jnp.sum(grad_out * normal, axis=0))


def wide_rows(values):
    return lax.all_gather(values, "wide", axis=0, tiled=True)


def wide_sums(values):
    return lax.psum_scatter(values, "wide", scatter_dimension=0, tiled=True)


def expert_trade(values):
    return lax.all_to_all(values, "wide", split_axis=0, concat_axis=0, tiled=True)


def expert_gather(values):
    return lax.all_gather(values, "rep", axis=0, tiled=True)


def expert_reduce(values):
    return lax.psum_scatter(
        values.astype(jnp.bfloat16), "rep", scatter_dimension=0, tiled=True
    ).astype(jnp.float32)


def across_section(values):
    return partner(values, "section", 0)


def attention_layout(packed, segment_ids):
    row_count = packed.shape[0]
    head_count = packed.shape[1] // (3 * HD)
    seq_count = row_count // SEQ_LEN
    block_rows = min(512, SEQ_LEN)
    per_seq = SEQ_LEN // block_rows
    head_parts = packed.reshape(seq_count, SEQ_LEN, head_count, 3, HD)
    seg_table = segment_ids.reshape(seq_count, SEQ_LEN)
    return (head_parts, seg_table, block_rows, per_seq, head_count, seq_count)


def block_scores(seq_parts, seq_segs, row_start, block_rows):
    key_end = row_start + block_rows
    queries = seq_parts[row_start:key_end, :, 0]
    scores = jnp.einsum(
        "qhd,khd->hqk", queries, seq_parts[:key_end, :, 1], preferred_element_type=jnp.float32
    ) * (1.0 / math.sqrt(HD))
    seg_query = seq_segs[row_start:key_end]
    query_pos = row_start + jnp.arange(block_rows, dtype=jnp.int32)
    key_pos = jnp.arange(key_end, dtype=jnp.int32)
    allowed = (query_pos[:, None] >= key_pos[None, :]) & (
        seg_query[:, None] == seq_segs[None, :key_end]
    )
    return (jnp.where(allowed[None], scores, masked_score), queries)


def attention_forward(packed, segment_ids):
    head_parts, seg_table, block_rows, per_seq, head_count, seq_count = attention_layout(
        packed, segment_ids
    )

    def one_seq(seq_pack):
        seq_parts, seq_segs = seq_pack
        block_outs, block_logs = ([], [])
        for block_no in range(per_seq):
            row_start = block_no * block_rows
            key_end = row_start + block_rows
            scores, queries = block_scores(seq_parts, seq_segs, row_start, block_rows)
            highest = jnp.max(scores, axis=-1, keepdims=True)
            exponent = jnp.exp(scores - highest)
            row_total = jnp.sum(exponent, axis=-1, keepdims=True)
            probs_low = (exponent / row_total).astype(jnp.bfloat16)
            attended = jnp.einsum(
                "hqk,khd->qhd",
                probs_low,
                seq_parts[:key_end, :, 2],
                preferred_element_type=jnp.float32,
            )
            block_outs.append(attended.astype(jnp.bfloat16).reshape(block_rows, head_count * HD))
            block_logs.append(highest[..., 0] + jnp.log(row_total[..., 0]))
        return (jnp.concatenate(block_outs, axis=0), jnp.stack(block_logs))

    attended, log_totals = lax.map(one_seq, (head_parts, seg_table))
    return (attended.reshape(packed.shape[0], head_count * HD), log_totals)


def attention_backward(packed, segment_ids, log_totals, grad_att):
    head_parts, seg_table, block_rows, per_seq, head_count, seq_count = attention_layout(
        packed, segment_ids
    )
    grad_seqs = grad_att.reshape(seq_count, SEQ_LEN, head_count, HD)
    scale_value = 1.0 / math.sqrt(HD)

    def one_seq(seq_pack):
        seq_parts, seq_segs, seq_logs, seq_grad = seq_pack
        query_list = []
        grad_key = jnp.zeros((SEQ_LEN, head_count, HD), jnp.float32)
        grad_value = jnp.zeros((SEQ_LEN, head_count, HD), jnp.float32)
        for block_no in range(per_seq):
            row_start = block_no * block_rows
            key_end = row_start + block_rows
            scores, queries = block_scores(seq_parts, seq_segs, row_start, block_rows)
            probs = jnp.exp(scores - seq_logs[block_no][..., None])
            grad_here = seq_grad[row_start:key_end]
            grad_probs = jnp.einsum(
                "qhd,khd->hqk",
                grad_here,
                seq_parts[:key_end, :, 2],
                preferred_element_type=jnp.float32,
            )
            inner = jnp.sum(grad_probs * probs, axis=-1, keepdims=True)
            grad_scores = (probs * (grad_probs - inner)).astype(jnp.bfloat16)
            query_list.append(
                jnp.einsum(
                    "hqk,khd->qhd",
                    grad_scores,
                    seq_parts[:key_end, :, 1],
                    preferred_element_type=jnp.float32,
                )
                * scale_value
            )
            key_part = (
                jnp.einsum("hqk,qhd->khd", grad_scores, queries, preferred_element_type=jnp.float32)
                * scale_value
            )
            value_part = jnp.einsum(
                "hqk,qhd->khd",
                probs.astype(jnp.bfloat16),
                grad_here,
                preferred_element_type=jnp.float32,
            )
            pad_rows = ((0, SEQ_LEN - key_end), (0, 0), (0, 0))
            grad_key = grad_key + jnp.pad(key_part, pad_rows)
            grad_value = grad_value + jnp.pad(value_part, pad_rows)
        return (jnp.concatenate(query_list, axis=0), grad_key, grad_value)

    grad_query, grad_key, grad_value = lax.map(
        one_seq, (head_parts, seg_table, log_totals, grad_seqs)
    )
    stacked = jnp.stack([grad_query, grad_key, grad_value], axis=3)
    return stacked.reshape(packed.shape[0], head_count * 3 * HD).astype(jnp.bfloat16)


def dense_forward(block_in, segment_ids, weights):
    first_norm_gain, qkv_mat, out_mat, second_norm_gain, up_mat, down_mat = weights
    shaped_one, normal_one, inv_one = norm_forward(block_in, first_norm_gain)
    normed_first = wide_rows(shaped_one.astype(jnp.bfloat16))
    packed = matmul(normed_first, qkv_mat).astype(jnp.bfloat16)
    attended, log_totals = attention_forward(packed, segment_ids)
    middle = block_in + wide_sums(matmul(attended, out_mat))
    shaped_two, normal_two, inv_two = norm_forward(middle, second_norm_gain)
    normed_second = wide_rows(shaped_two.astype(jnp.bfloat16))
    pre_act = matmul(normed_second, up_mat)
    activated = gelu_curve(pre_act).astype(jnp.bfloat16)
    dense_output = middle + wide_sums(matmul(activated, down_mat))
    return (
        dense_output,
        (
            normal_one,
            inv_one,
            normed_first,
            packed,
            attended,
            log_totals,
            normal_two,
            inv_two,
            normed_second,
            pre_act,
            activated,
        ),
    )


def dense_backward(grad_out, saved_state, segment_ids, weights):
    first_norm_gain, qkv_mat, out_mat, second_norm_gain, up_mat, down_mat = weights
    (
        normal_one,
        inv_one,
        normed_first,
        packed,
        attended,
        log_totals,
        normal_two,
        inv_two,
        normed_second,
        pre_act,
        activated,
    ) = saved_state
    grad_wide = wide_rows(grad_out.astype(jnp.bfloat16))
    grad_down = matmul_left(activated, grad_wide)
    grad_act = matmul_right(grad_wide, down_mat)
    grad_pre = (grad_act * gelu_slope(pre_act)).astype(jnp.bfloat16)
    grad_up = matmul_left(normed_second, grad_pre)
    grad_norm_two = wide_sums(matmul_right(grad_pre, up_mat))
    grad_in_two, grad_gain_two = norm_backward(grad_norm_two, normal_two, inv_two, second_norm_gain)
    grad_middle = grad_out + grad_in_two
    grad_mid_wide = wide_rows(grad_middle.astype(jnp.bfloat16))
    grad_out_mat = matmul_left(attended, grad_mid_wide)
    grad_att = matmul_right(grad_mid_wide, out_mat).astype(jnp.bfloat16)
    grad_packed = attention_backward(packed, segment_ids, log_totals, grad_att)
    grad_qkv = matmul_left(normed_first, grad_packed)
    grad_norm_one = wide_sums(matmul_right(grad_packed, qkv_mat))
    grad_in_one, grad_gain_one = norm_backward(grad_norm_one, normal_one, inv_one, first_norm_gain)
    return (
        grad_middle + grad_in_one,
        (grad_gain_one, grad_qkv, grad_out_mat, grad_gain_two, grad_up, grad_down),
    )


def slot_matrix_of(route_ids):
    expert_count = lax.axis_size("wide")
    capacity = max(2, route_ids.shape[0] // expert_count)
    onehot = (route_ids[:, None] == jnp.arange(expert_count, dtype=jnp.int32)[None, :]).astype(
        jnp.int32
    )
    rank_ids = jnp.sum(jnp.cumsum(onehot, axis=0) * onehot, axis=1) - 1
    position = route_ids * capacity + rank_ids
    return (
        position[:, None] == jnp.arange(expert_count * capacity, dtype=jnp.int32)[None, :]
    ).astype(jnp.bfloat16)


def expert_forward(dense_output, route_ids, centroid, gain_rows, up_mats, down_mats):
    slot_matrix = slot_matrix_of(route_ids)
    outgoing = matmul_left(slot_matrix, dense_output.astype(jnp.bfloat16)).astype(jnp.bfloat16)
    arrived = expert_trade(outgoing)
    starting_rows = arrived.astype(jnp.float32)
    gate_value = jax.nn.sigmoid(jnp.dot(arrived, centroid, preferred_element_type=jnp.float32))
    current = starting_rows
    sublayer_saved = []
    for sublayer in range(2):
        shaped, normal, scale_inv = norm_forward(current, gain_rows[sublayer])
        gathered = expert_gather(shaped.astype(jnp.bfloat16))
        pre_act = matmul(gathered, up_mats[sublayer])
        activated = gelu_curve(pre_act).astype(jnp.bfloat16)
        branch = expert_reduce(matmul(activated, down_mats[sublayer]))
        sublayer_saved.append((normal, scale_inv, gathered, pre_act, activated))
        current = current + branch
    mixed_rows = gate_value[:, None] * current + (1.0 - gate_value[:, None]) * starting_rows
    returned = expert_trade(mixed_rows.astype(jnp.bfloat16))
    return (
        matmul(slot_matrix, returned),
        (slot_matrix, arrived, gate_value, current, tuple(sublayer_saved)),
    )


def expert_backward(grad_tokens, saved_state, centroid, gain_rows, up_mats, down_mats):
    slot_matrix, arrived, gate_value, final_state, sublayer_saved = saved_state
    starting_rows = arrived.astype(jnp.float32)
    outgoing = matmul_left(slot_matrix, grad_tokens).astype(jnp.bfloat16)
    grad_mixed = expert_trade(outgoing).astype(jnp.float32)
    grad_gate = jnp.sum(grad_mixed * (final_state - starting_rows), axis=-1)
    grad_logit = grad_gate * gate_value * (1.0 - gate_value)
    grad_centroid = jnp.dot(grad_logit, starting_rows, precision=highest_prec)
    grad_state = gate_value[:, None] * grad_mixed
    grad_start = (1.0 - gate_value[:, None]) * grad_mixed + grad_logit[:, None] * centroid.astype(
        jnp.float32
    )[None, :]
    gain_list, up_list, down_list = ([], [], [])
    for sublayer in (1, 0):
        normal, scale_inv, gathered, pre_act, activated = sublayer_saved[sublayer]
        grad_wide = expert_gather(grad_state.astype(jnp.bfloat16))
        down_list.append(matmul_left(activated, grad_wide))
        grad_act = matmul_right(grad_wide, down_mats[sublayer])
        grad_pre = (grad_act * gelu_slope(pre_act)).astype(jnp.bfloat16)
        up_list.append(matmul_left(gathered, grad_pre))
        grad_normed = expert_reduce(matmul_right(grad_pre, up_mats[sublayer]))
        grad_values, grad_gain = norm_backward(grad_normed, normal, scale_inv, gain_rows[sublayer])
        gain_list.append(grad_gain)
        grad_state = grad_state + grad_values
    grad_start = grad_start + grad_state
    returned = expert_trade(grad_start.astype(jnp.bfloat16))
    grad_input = matmul(slot_matrix, returned)
    grad_parts = (
        grad_centroid,
        jnp.stack(gain_list[::-1]),
        jnp.stack(up_list[::-1]),
        jnp.stack(down_list[::-1]),
    )
    return (grad_input, grad_parts)


def layer_forward(block_in, segment_ids, route_ids, dense_weights, expert_weights):
    dense_output, dense_saved = dense_forward(block_in, segment_ids, dense_weights)
    layer_out, expert_saved = expert_forward(dense_output, route_ids, *expert_weights)
    return (layer_out, (dense_saved, expert_saved))


def layer_backward(grad_out, saved_state, segment_ids, dense_weights, expert_weights):
    grad_mid, expert_grads = expert_backward(grad_out, saved_state[1], *expert_weights)
    grad_in, dense_grads = dense_backward(grad_mid, saved_state[0], segment_ids, dense_weights)
    return (grad_in, dense_grads + expert_grads)


def shards(
    tokens_in,
    cotangent,
    segments,
    routes,
    ln1_gain,
    w_qkv,
    w_out,
    ln2_gain,
    w_up,
    w_down,
    centroids,
    sub_gains,
    expert_up,
    expert_down,
):
    section_index = lax.axis_index("section")
    is_first = section_index == 0
    micro_count = tokens_in.shape[0]
    out_mat = w_out[0]
    dense_weights = (ln1_gain[0], w_qkv[0], out_mat, ln2_gain[0], w_up[0], w_down[0])
    expert_weights = (centroids[0, 0], sub_gains[0, 0], expert_up[0, 0], expert_down[0, 0])
    route_table = routes[0, :, :, 0]
    received = jnp.zeros(tokens_in.shape[1:], jnp.float32)
    inputs, keep_all, outputs = ([], [], [])
    for tick_no in range(micro_count + 1):
        batch_no = jnp.clip(tick_no - section_index, 0, micro_count - 1)
        block_in = jnp.where(
            is_first, tokens_in[min(tick_no, micro_count - 1)].astype(jnp.float32), received
        )
        segment_ids = lax.dynamic_index_in_dim(segments, batch_no, 0, keepdims=False)
        route_ids = lax.dynamic_index_in_dim(route_table, batch_no, 0, keepdims=False)
        layer_out, saved_state = layer_forward(
            block_in, segment_ids, route_ids, dense_weights, expert_weights
        )
        inputs.append(block_in)
        keep_all.append(saved_state)
        outputs.append(layer_out)
        if tick_no < micro_count:
            received = across_section(layer_out.astype(jnp.bfloat16)).astype(jnp.float32)
    stacked = jax.tree.map(lambda *leaves: jnp.stack(leaves), *keep_all)
    grad_received = jnp.zeros(tokens_in.shape[1:], jnp.bfloat16)
    grad_totals = None
    input_grads = []
    for tick_no in range(micro_count + 1):
        batch_no = jnp.clip(tick_no - 1 + section_index, 0, micro_count - 1)
        saved_no = jnp.clip(tick_no - 1 + 2 * section_index, 0, micro_count)
        valid_flag = jnp.where(is_first, tick_no >= 1, tick_no < micro_count).astype(jnp.float32)
        segment_ids = lax.dynamic_index_in_dim(segments, batch_no, 0, keepdims=False)
        route_ids = lax.dynamic_index_in_dim(route_table, batch_no, 0, keepdims=False)
        saved_state = jax.tree.map(
            lambda leaf_arr: lax.dynamic_index_in_dim(leaf_arr, saved_no, 0, keepdims=False),
            stacked,
        )
        grad_out = jnp.where(is_first, grad_received, cotangent[min(tick_no, micro_count - 1)])
        grad_in, grad_parts = layer_backward(
            grad_out, saved_state, segment_ids, dense_weights, expert_weights
        )
        scaled = jax.tree.map(lambda part_arr: part_arr * valid_flag, grad_parts)
        grad_totals = scaled if grad_totals is None else jax.tree.map(jnp.add, grad_totals, scaled)
        input_grads.append(grad_in)
        if tick_no < micro_count:
            grad_received = across_section(grad_in.astype(jnp.bfloat16))
    produced = jnp.stack(outputs[1:])
    input_grad = jnp.stack(input_grads[1:])
    half_width = produced.shape[2] // 2
    outgoing = jnp.where(is_first, input_grad[:, :, half_width:], produced[:, :, :half_width])
    incoming = partner(shortened(outgoing), "section", 0).astype(outgoing.dtype)
    block_out = jnp.where(is_first, incoming, produced[:, :, half_width:]).astype(jnp.bfloat16)
    grad_input = jnp.where(is_first, input_grad[:, :, :half_width], incoming)
    (
        gain_first_grad,
        qkv_grad,
        out_grad,
        gain_second_grad,
        up_grad,
        down_grad,
        centroid_grad,
        sub_gain_grad,
        expert_up_grad,
        expert_down_grad,
    ) = grad_totals
    gain_sums = lax.psum_scatter(
        jnp.stack([gain_first_grad, gain_second_grad]),
        ("wide", "rep"),
        scatter_dimension=1,
        tiled=True,
    )
    qkv_grad, out_grad, up_grad, down_grad, centroid_grad, sub_gain_grad = (
        lax.psum_scatter(
            qkv_grad.astype(jnp.bfloat16), "rep", scatter_dimension=0, tiled=True
        ).astype(jnp.float32),
        lax.psum_scatter(
            out_grad.astype(jnp.bfloat16), "rep", scatter_dimension=1, tiled=True
        ).astype(jnp.float32),
        lax.psum_scatter(
            up_grad.astype(jnp.bfloat16), "rep", scatter_dimension=0, tiled=True
        ).astype(jnp.float32),
        lax.psum_scatter(
            down_grad.astype(jnp.bfloat16), "rep", scatter_dimension=1, tiled=True
        ).astype(jnp.float32),
        lax.psum_scatter(
            centroid_grad.astype(jnp.bfloat16), "rep", scatter_dimension=0, tiled=True
        ).astype(jnp.float32),
        lax.psum_scatter(
            sub_gain_grad.astype(jnp.bfloat16), "rep", scatter_dimension=1, tiled=True
        ).astype(jnp.float32),
    )
    return (
        block_out,
        grad_input,
        gain_sums[0][None],
        qkv_grad[None],
        out_grad[None],
        gain_sums[1][None],
        up_grad[None],
        down_grad[None],
        centroid_grad[None, None],
        sub_gain_grad[None, None],
        expert_up_grad[None, None],
        expert_down_grad[None, None],
    )


def solution(mesh):
    in_specs = (
        P(None, ("rep", "wide"), None),
        P(None, ("rep", "wide"), None),
        P(None, "rep"),
        P("section", None, ("rep", "wide"), None),
        P("section", None),
        P("section", None, "wide"),
        P("section", "wide", None),
        P("section", None),
        P("section", None, "wide"),
        P("section", "wide", None),
        P("section", "wide", None),
        P("section", "wide", None, None),
        P("section", "wide", None, None, "rep"),
        P("section", "wide", None, "rep", None),
    )
    out_specs = (
        P(None, ("rep", "wide"), "section"),
        P(None, ("rep", "wide"), "section"),
        P("section", ("wide", "rep")),
        P("section", "rep", "wide"),
        P("section", "wide", "rep"),
        P("section", ("wide", "rep")),
        P("section", "rep", "wide"),
        P("section", "wide", "rep"),
        P("section", "wide", "rep"),
        P("section", "wide", None, "rep"),
        P("section", "wide", None, None, "rep"),
        P("section", "wide", None, "rep", None),
    )
    return jax.shard_map(shards, mesh=mesh, in_specs=in_specs, out_specs=out_specs, check_vma=False)
```

profile of v0, /device:TPU:0, one launch (start us, length us, event | category | flops | bytes accessed | tf_op | source)
XLA Modules:
  0.0 2920.7 jit_solution(1903579293335270846)
XLA Ops:
  68.4 52.4 %reduce-scatter.35.cloned.1.call-done = f32[256,1024]{1,0:T(8,128)} async-done(((f32[1024,1024]{1,0:T(8,128)}), f32[256,1024]{1,0:T(8,128)}) %reduce-scatter.35.cloned.1.call-update) | async-done | bytes 1048592 | tf_op jit(solution)/shard_map/reduce_scatter | solution.py:82
  174.0 50.6 %reduce-scatter.37.cloned.1.call-done = f32[256,1024]{1,0:T(8,128)} async-done(((f32[1024,1024]{1,0:T(8,128)}), f32[256,1024]{1,0:T(8,128)}) %reduce-scatter.37.cloned.1.call-update) | async-done | bytes 1048592 | tf_op jit(solution)/shard_map/reduce_scatter | solution.py:82
  240.5 46.0 %all-gather.29.cloned.1.call-done = bf16[1024,1024]{1,0:T(8,128)(2,1)} async-done(((bf16[256,1024]{1,0:T(8,128)(2,1)}), bf16[1024,1024]{1,0:T(8,128)(2,1)}) %all-gather.29.cloned.1.call-update) | async-done | bytes 2097168 | tf_op jit(solution)/shard_map/all_gather | solution.py:90
  298.5 42.7 %reduce-scatter.39.cloned.1.call-done = bf16[256,1024]{1,0:T(8,128)(2,1)} async-done(((bf16[1024,1024]{1,0:T(8,128)(2,1)}), bf16[256,1024]{1,0:T(8,128)(2,1)}) %reduce-scatter.39.cloned.1.call-update) | async-done | bytes 524304 | tf_op jit(solution)/shard_map/reduce_scatter | solution.py:94
  346.3 45.4 %all-gather.31.cloned.1.call-done = bf16[1024,1024]{1,0:T(8,128)(2,1)} async-done(((bf16[256,1024]{1,0:T(8,128)(2,1)}), bf16[1024,1024]{1,0:T(8,128)(2,1)}) %all-gather.31.cloned.1.call-update) | async-done | bytes 2097168 | tf_op jit(solution)/shard_map/all_gather | solution.py:90
  515.6 52.8 %reduce-scatter.43.cloned.1.call-done = f32[256,1024]{1,0:T(8,128)} async-done(((f32[1024,1024]{1,0:T(8,128)}), f32[256,1024]{1,0:T(8,128)}) %reduce-scatter.43.cloned.1.call-update) | async-done | bytes 1048592 | tf_op jit(solution)/shard_map/reduce_scatter | solution.py:82
  621.3 51.1 %reduce-scatter.45.cloned.1.call-done = f32[256,1024]{1,0:T(8,128)} async-done(((f32[1024,1024]{1,0:T(8,128)}), f32[256,1024]{1,0:T(8,128)}) %reduce-scatter.45.cloned.1.call-update) | async-done | bytes 1048592 | tf_op jit(solution)/shard_map/reduce_scatter | solution.py:82
  687.1 45.5 %all-gather.37.cloned.1.call-done = bf16[1024,1024]{1,0:T(8,128)(2,1)} async-done(((bf16[256,1024]{1,0:T(8,128)(2,1)}), bf16[1024,1024]{1,0:T(8,128)(2,1)}) %all-gather.37.cloned.1.call-update) | async-done | bytes 2097168 | tf_op jit(solution)/shard_map/all_gather | solution.py:90
  744.6 42.7 %reduce-scatter.47.cloned.1.call-done = bf16[256,1024]{1,0:T(8,128)(2,1)} async-done(((bf16[1024,1024]{1,0:T(8,128)(2,1)}), bf16[256,1024]{1,0:T(8,128)(2,1)}) %reduce-scatter.47.cloned.1.call-update) | async-done | bytes 524304 | tf_op jit(solution)/shard_map/reduce_scatter | solution.py:94
  792.4 45.4 %all-gather.39.cloned.1.call-done = bf16[1024,1024]{1,0:T(8,128)(2,1)} async-done(((bf16[256,1024]{1,0:T(8,128)(2,1)}), bf16[1024,1024]{1,0:T(8,128)(2,1)}) %all-gather.39.cloned.1.call-update) | async-done | bytes 2097168 | tf_op jit(solution)/shard_map/all_gather | solution.py:90
  962.7 52.8 %reduce-scatter.51.cloned.1.call-done = f32[256,1024]{1,0:T(8,128)} async-done(((f32[1024,1024]{1,0:T(8,128)}), f32[256,1024]{1,0:T(8,128)}) %reduce-scatter.51.cloned.1.call-update) | async-done | bytes 1048592 | tf_op jit(solution)/shard_map/reduce_scatter | solution.py:82
  1068.2 51.1 %reduce-scatter.53.cloned.1.call-done = f32[256,1024]{1,0:T(8,128)} async-done(((f32[1024,1024]{1,0:T(8,128)}), f32[256,1024]{1,0:T(8,128)}) %reduce-scatter.53.cloned.1.call-update) | async-done | bytes 1048592 | tf_op jit(solution)/shard_map/reduce_scatter | solution.py:82
  1134.3 45.5 %all-gather.45.cloned.1.call-done = bf16[1024,1024]{1,0:T(8,128)(2,1)} async-done(((bf16[256,1024]{1,0:T(8,128)(2,1)}), bf16[1024,1024]{1,0:T(8,128)(2,1)}) %all-gather.45.cloned.1.call-update) | async-done | bytes 2097168 | tf_op jit(solution)/shard_map/all_gather | solution.py:90
  1191.7 42.7 %reduce-scatter.55.cloned.1.call-done = bf16[256,1024]{1,0:T(8,128)(2,1)} async-done(((bf16[1024,1024]{1,0:T(8,128)(2,1)}), bf16[256,1024]{1,0:T(8,128)(2,1)}) %reduce-scatter.55.cloned.1.call-update) | async-done | bytes 524304 | tf_op jit(solution)/shard_map/reduce_scatter | solution.py:94
  1595.5 47.6 %reduce-scatter.63.cloned.1.call-done = f32[256,1024]{1,0:T(8,128)} async-done(((f32[1024,1024]{1,0:T(8,128)}), f32[256,1024]{1,0:T(8,128)}) %reduce-scatter.63.cloned.1.call-update) | async-done | bytes 1048592 | tf_op jit(solution)/shard_map/reduce_scatter | solution.py:82
  1713.9 47.1 %reduce-scatter.65.cloned.1.call-done = f32[256,1024]{1,0:T(8,128)} async-done(((f32[1024,1024]{1,0:T(8,128)}), f32[256,1024]{1,0:T(8,128)}) %reduce-scatter.65.cloned.1.call-update) | async-done | bytes 1048592 | tf_op jit(solution)/shard_map/reduce_scatter | solution.py:82
  1780.3 45.5 %all-gather.57.cloned.1.call-done = bf16[1024,1024]{1,0:T(8,128)(2,1)} async-done(((bf16[256,1024]{1,0:T(8,128)(2,1)}), bf16[1024,1024]{1,0:T(8,128)(2,1)}) %all-gather.57.cloned.1.call-update) | async-done | bytes 2097168 | tf_op jit(solution)/shard_map/all_gather | solution.py:90
  1884.9 45.4 %all-gather.59.cloned.1.call-done = bf16[1024,1024]{1,0:T(8,128)(2,1)} async-done(((bf16[256,1024]{1,0:T(8,128)(2,1)}), bf16[1024,1024]{1,0:T(8,128)(2,1)}) %all-gather.59.cloned.1.call-update) | async-done | bytes 2097168 | tf_op jit(solution)/shard_map/all_gather | solution.py:90
  2047.5 52.8 %reduce-scatter.71.cloned.1.call-done = f32[256,1024]{1,0:T(8,128)} async-done(((f32[1024,1024]{1,0:T(8,128)}), f32[256,1024]{1,0:T(8,128)}) %reduce-scatter.71.cloned.1.call-update) | async-done | bytes 1048592 | tf_op jit(solution)/shard_map/reduce_scatter | solution.py:82
  2165.5 52.8 %reduce-scatter.73.cloned.1.call-done = f32[256,1024]{1,0:T(8,128)} async-done(((f32[1024,1024]{1,0:T(8,128)}), f32[256,1024]{1,0:T(8,128)}) %reduce-scatter.73.cloned.1.call-update) | async-done | bytes 1048592 | tf_op jit(solution)/shard_map/reduce_scatter | solution.py:82
  2238.5 45.5 %all-gather.65.cloned.1.call-done = bf16[1024,1024]{1,0:T(8,128)(2,1)} async-done(((bf16[256,1024]{1,0:T(8,128)(2,1)}), bf16[1024,1024]{1,0:T(8,128)(2,1)}) %all-gather.65.cloned.1.call-update) | async-done | bytes 2097168 | tf_op jit(solution)/shard_map/all_gather | solution.py:90
  2295.4 42.7 %reduce-scatter.75.cloned.1.call-done = bf16[256,1024]{1,0:T(8,128)(2,1)} async-done(((bf16[1024,1024]{1,0:T(8,128)(2,1)}), bf16[256,1024]{1,0:T(8,128)(2,1)}) %reduce-scatter.75.cloned.1.call-update) | async-done | bytes 524304 | tf_op jit(solution)/shard_map/reduce_scatter | solution.py:94
  2342.6 45.4 %all-gather.67.cloned.1.call-done = bf16[1024,1024]{1,0:T(8,128)(2,1)} async-done(((bf16[256,1024]{1,0:T(8,128)(2,1)}), bf16[1024,1024]{1,0:T(8,128)(2,1)}) %all-gather.67.cloned.1.call-update) | async-done | bytes 2097168 | tf_op jit(solution)/shard_map/all_gather | solution.py:90
  2829.9 76.9 %reduce-scatter.91.cloned.1.call-done = f32[64,2]{1,0:T(8,128)} async-done(((f32[1024,2]{1,0:T(8,128)}), f32[64,2]{1,0:T(8,128)}) %reduce-scatter.91.cloned.1.call-update) | async-done | bytes 528
  (1047 shorter events, 1733.5 us)
Async XLA Ops:
  12.6 108.2 %reduce-scatter.35.cloned.1.call-start = ((), (), s32[]{:S(2)}) async-start(), calls=%async_computation.43 | async-start | bytes 5242880 | tf_op jit(solution)/shard_map/reduce_scatter | solution.py:82
  240.4 100.7 %reduce-scatter.39.cloned.1.call-start = ((), (), s32[]{:S(2)}) async-start(), calls=%async_computation.47 | async-start | bytes 2621440 | tf_op jit(solution)/shard_map/reduce_scatter | solution.py:94
  464.8 103.6 %reduce-scatter.43.cloned.1.call-start = ((), (), s32[]{:S(2)}) async-start(), calls=%async_computation.51 | async-start | bytes 5242880 | tf_op jit(solution)/shard_map/reduce_scatter | solution.py:82
  619.6 113.0 %all-gather.37.cloned.1.call-start = ((), (), s32[]{:S(2)}) async-start(), calls=%async_computation.54 | async-start | bytes 2621440 | tf_op jit(solution)/shard_map/all_gather | solution.py:90
  687.0 100.2 %reduce-scatter.47.cloned.1.call-start = ((), (), s32[]{:S(2)}) async-start(), calls=%async_computation.55 | async-start | bytes 2621440 | tf_op jit(solution)/shard_map/reduce_scatter | solution.py:94
  792.4 100.1 %reduce-scatter.49.cloned.1.call-start = ((), (), s32[]{:S(2)}) async-start(), calls=%async_computation.57 | async-start | bytes 2621440 | tf_op jit(solution)/shard_map/reduce_scatter | solution.py:94
  911.8 103.7 %reduce-scatter.51.cloned.1.call-start = ((), (), s32[]{:S(2)}) async-start(), calls=%async_computation.59 | async-start | bytes 5242880 | tf_op jit(solution)/shard_map/reduce_scatter | solution.py:82
  1066.5 113.3 %all-gather.45.cloned.1.call-start = ((), (), s32[]{:S(2)}) async-start(), calls=%async_computation.62 | async-start | bytes 2621440 | tf_op jit(solution)/shard_map/all_gather | solution.py:90
  1134.3 100.2 %reduce-scatter.55.cloned.1.call-start = ((), (), s32[]{:S(2)}) async-start(), calls=%async_computation.63 | async-start | bytes 2621440 | tf_op jit(solution)/shard_map/reduce_scatter | solution.py:94
  1256.4 128.7 %reduce-scatter.59.cloned.1.call-start = ((), (), s32[]{:S(2)}) async-start(), calls=%async_computation.67 | async-start | bytes 2621440 | tf_op jit(solution)/shard_map/reduce_scatter | solution.py:94
  1396.2 130.4 %reduce-scatter.61.cloned.1.call-start = ((), (), s32[]{:S(2)}) async-start(), calls=%async_computation.69 | async-start | bytes 2621440 | tf_op jit(solution)/shard_map/reduce_scatter | solution.py:94
  1447.1 131.0 %all-gather.53.cloned.1.call-start = ((), (), s32[]{:S(2)}) async-start(), calls=%async_computation.70 | async-start | bytes 2621440 | tf_op jit(solution)/shard_map/all_gather | solution.py:78
  1648.6 112.4 %reduce-scatter.65.cloned.1.call-start = ((), (), s32[]{:S(2)}) async-start(), calls=%async_computation.73 | async-start | bytes 5242880 | tf_op jit(solution)/shard_map/reduce_scatter | solution.py:82
  1708.2 117.6 %all-gather.57.cloned.1.call-start = ((), (), s32[]{:S(2)}) async-start(), calls=%async_computation.74 | async-start | bytes 2621440 | tf_op jit(solution)/shard_map/all_gather | solution.py:90
  2105.8 112.5 %reduce-scatter.73.cloned.1.call-start = ((), (), s32[]{:S(2)}) async-start(), calls=%async_computation.81 | async-start | bytes 5242880 | tf_op jit(solution)/shard_map/reduce_scatter | solution.py:82
  2165.4 118.6 %all-gather.65.cloned.1.call-start = ((), (), s32[]{:S(2)}) async-start(), calls=%async_computation.82 | async-start | bytes 2621440 | tf_op jit(solution)/shard_map/all_gather | solution.py:90
  2505.1 152.3 %all-gather.71.cloned.1.call-start = ((), (), s32[]{:S(2)}) async-start(), calls=%async_computation.88 | async-start | bytes 2621440 | tf_op jit(solution)/shard_map/all_gather | solution.py:78
  2563.5 245.7 %reduce-scatter.93.cloned.1.call-start = ((), (), s32[]{:S(2)}) async-start(), calls=%async_computation.95 | async-start | bytes 327680
  2601.7 209.1 %reduce-scatter.87.cloned.1.call-start = ((), (), s32[]{:S(2)}) async-start(), calls=%async_computation.92 | async-start | bytes 2621440 | tf_op jit(solution)/shard_map/reduce_scatter | solution.py:462
  2630.0 182.9 %reduce-scatter.89.cloned.1.call-start = ((), (), s32[]{:S(2)}) async-start(), calls=%async_computation.93 | async-start | bytes 2621440 | tf_op jit(solution)/shard_map/reduce_scatter | solution.py:465
  2657.1 158.0 %reduce-scatter.85.cloned.1.call-start = ((), (), s32[]{:S(2)}) async-start(), calls=%async_computation.91 | async-start | bytes 655360 | tf_op jit(solution)/shard_map/reduce_scatter | solution.py:459
  2686.4 130.3 %reduce-scatter.81.cloned.1.call-start = ((), (), s32[]{:S(2)}) async-start(), calls=%async_computation.89 | async-start | bytes 5242880 | tf_op jit(solution)/shard_map/reduce_scatter | solution.py:82
  2696.3 131.7 %reduce-scatter.83.cloned.1.call-start = ((), (), s32[]{:S(2)}) async-start(), calls=%async_computation.90 | async-start | bytes 1966080 | tf_op jit(solution)/shard_map/reduce_scatter | solution.py:456
  2795.2 111.7 %reduce-scatter.91.cloned.1.call-start = ((), (), s32[]{:S(2)}) async-start(), calls=%async_computation.94 | async-start | bytes 557056
  (268 other events, 6560.7 us)
Sparse Core Ops, SparseCore 0:
  68.1 52.6 reduce-scatter.34
  171.8 52.6 reduce-scatter.36
  240.6 45.9 all-gather.28
  346.4 45.2 all-gather.30
  515.7 52.6 reduce-scatter.42
  619.7 52.6 reduce-scatter.44
  687.1 45.3 all-gather.36
  792.5 45.2 all-gather.38
  962.7 52.6 reduce-scatter.50
  1066.6 52.6 reduce-scatter.52
  1134.4 45.3 all-gather.44
  1239.7 45.2 all-gather.46
  1390.4 45.2 all-gather.50
  1590.4 52.6 reduce-scatter.62
  1708.3 52.6 reduce-scatter.64
  1780.4 45.3 all-gather.56
  1885.0 45.2 all-gather.58
  2047.6 52.6 reduce-scatter.70
  2165.5 52.6 reduce-scatter.72
  2238.5 45.3 all-gather.64
  2342.6 45.2 all-gather.66
  2505.3 52.6 reduce-scatter.78
  2738.3 50.9 reduce-scatter.80
  2830.9 75.8 reduce-scatter.90
  (30 shorter events, 1129.9 us)
where the time goes:
time: 2930 us; the launch traced here: 2920 us
  waiting for transfers between devices  1980 us (68%)
  matrix products  458 us (16%)
  other arithmetic  271 us (9%)
  blocking collectives  116 us (4%)
  local copies, waits for them, and re-layouts  61.5 us (2%)
    reduce_scatter x12, waiting for transfers between devices, wide_sums(): return lax.psum_scatter(values, 'wide', scatter_dimension=0, tiled=True)  545 us
    all_gather x12, waiting for transfers between devices, expert_gather(): return lax.all_gather(values, 'rep', axis=0, tiled=True)  501 us
    reduce_scatter x12, waiting for transfers between devices, expert_reduce(): lax.psum_scatter(values.astype(jnp.bfloat16), 'rep', scatter_dimension=0,...  482 us
    all_gather x12, waiting for transfers between devices, wide_rows(): return lax.all_gather(values, 'wide', axis=0, tiled=True)  341 us
    dot_general x30, matrix products, matmul_left(): lax.dot_general(first_arg, second_arg, (((0,), (0,)), ((), ())), preferre...  132 us
    dot_general x30, matrix products, matmul(): return jnp.dot(first_arg, second_arg, preferred_element_type=jnp.float32)  120 us
    dot_general x24, matrix products, matmul_right(): lax.dot_general(first_arg, second_arg, (((1,), (1,)), ((), ())), preferre...  112 us
    all_to_all x9, blocking collectives, expert_trade(): lax.all_to_all(values, 'wide', split_axis=0, concat_axis=0, tiled=True)  104 us
  transfers between devices with their start and end apart: 62, of which 55 were waited for; matrix products, arithmetic and copies ran while one was open for 13% of the time, Pallas kernels for 0%

commit v1 on v0

v1 whole, which is shorter than its diff:
```python
import functools
import math

import jax
import jax.numpy as jnp
from jax import lax
from jax.experimental import pallas as pl
from jax.experimental.pallas import tpu as pltpu
from jax.sharding import PartitionSpec as P

HD = 64
SEQ_LEN = 1024


epsilon = 1e-05
root_half = 1.0 / math.sqrt(2.0)
root_tau = 1.0 / math.sqrt(2.0 * math.pi)
masked_score = -1e30
highest_prec = lax.Precision.HIGHEST


def section_swap(value):
    return lax.ppermute(value, "section", [(0, 1), (1, 0)])


def section_send(value, source):
    return lax.ppermute(value, "section", [(source, 1 - source)])


def together(values):
    return lax.optimization_barrier(values)


def after(value, earlier):
    return lax.optimization_barrier((value, earlier))[0]


def low(value):
    return value.astype(jnp.bfloat16)


def matmul(first_arg, second_arg):
    return jnp.dot(first_arg, second_arg, preferred_element_type=jnp.float32)


def matmul_left(first_arg, second_arg):
    return lax.dot_general(
        first_arg, second_arg, (((0,), (0,)), ((), ())), preferred_element_type=jnp.float32
    )


def matmul_right(first_arg, second_arg):
    return lax.dot_general(
        first_arg, second_arg, (((1,), (1,)), ((), ())), preferred_element_type=jnp.float32
    )


def hidden_tile(width):
    return min(512, width)


def row_steps(rows):
    step = min(256, rows)
    return [pl.ds(i, step) for i in range(0, rows, step)]


def store_parts(total, parts):
    size = parts[0].shape[0]
    for i, part in enumerate(parts):
        part[...] = total[pl.ds(i * size, size), :].astype(part.dtype)


def on_each_set(sets, steps, work):
    if len(sets) == 1:
        work(*sets[0])
        return
    for i, tiles in enumerate(sets):

        @pl.when(pl.program_id(0) // steps == i)
        def _(tiles=tiles):
            work(*tiles)


def mlp_forward_kernel(count, moves, sets, set_steps, *refs):
    blocks, refs = refs[:count], refs[count:]
    weights, refs = refs[: 2 * sets], refs[2 * sets :]
    weights = list(zip(weights[::2], weights[1::2]))
    if moves:
        moving, own_moving, middle, refs = refs[0], refs[1], refs[2], refs[3:]
    act, slope, rows_out = refs[:3]
    parts, total = refs[3:-1], refs[-1]
    step = pl.program_id(0)
    size = blocks[0].shape[0]
    steps = row_steps(total.shape[0])

    @pl.when(step == 0)
    def _():
        for i in range(count):
            rows_out[pl.ds(i * size, size), :] = blocks[i][...]
        if moves:
            for span in steps:
                total[span, :] = matmul(own_moving[span, :], middle[...])
        else:
            total[...] = jnp.zeros_like(total)

    def work(up_tile, down_tile):
        for span in steps:
            pre = matmul(rows_out[span, :], up_tile[...])
            below = 0.5 * (1.0 + lax.erf(pre * root_half))
            act[span, :] = low(pre * below)
            slope[span, :] = low(below + pre * (jnp.exp(-0.5 * pre * pre) * root_tau))
            if not moves:
                total[span, :] += matmul(act[span, :], down_tile[...])
        if moves:
            for span in steps:
                total[span, :] += matmul(low(matmul(moving[span, :], act[...])), down_tile[...])

    on_each_set(weights, set_steps, work)

    @pl.when(step == pl.num_programs(0) - 1)
    def _():
        store_parts(total, parts)


def mlp_backward_kernel(count, moves, sets, set_steps, *refs):
    blocks, slope, refs = refs[:count], refs[count], refs[count + 1 :]
    weights, refs = refs[: 2 * sets], refs[2 * sets :]
    weights = list(zip(weights[::2], weights[1::2]))
    if moves:
        moving, refs = refs[0], refs[1:]
    grad_pre, rows_out = refs[:2]
    parts, total = refs[2:-1], refs[-1]
    size = blocks[0].shape[0]
    steps = row_steps(total.shape[0])

    @pl.when(pl.program_id(0) == 0)
    def _():
        if moves:
            for span in steps:
                moved = jnp.zeros((span.size, total.shape[1]), jnp.float32)
                for i in range(count):
                    moved += matmul_left(moving[pl.ds(i * size, size), span], blocks[i][...])
                rows_out[span, :] = low(moved)
        else:
            for i in range(count):
                rows_out[pl.ds(i * size, size), :] = blocks[i][...]
        total[...] = jnp.zeros_like(total)

    def work(up_tile, down_tile):
        for span in steps:
            grad_act = matmul_right(rows_out[span, :], down_tile[...])
            grad_pre[span, :] = low(grad_act * slope[span, :].astype(jnp.float32))
            total[span, :] += matmul_right(grad_pre[span, :], up_tile[...])

    on_each_set(weights, set_steps, work)

    @pl.when(pl.program_id(0) == pl.num_programs(0) - 1)
    def _():
        store_parts(total, parts)


def mlp_call(kernel, blocks, streamed, resident, hidden_outs, weights):
    count, size = len(blocks), blocks[0].shape[0]
    rows, width = count * size, blocks[0].shape[1]
    set_width = weights[0][0].shape[-1]
    hidden = set_width * len(weights)
    tile = hidden_tile(set_width)
    set_steps = set_width // tile

    def whole(shape):
        return pl.BlockSpec(shape, lambda i: (0,) * len(shape))

    def tiles(lead, set_no, along_rows):
        def index(i):
            turn = jnp.clip(i - set_no * set_steps, 0, set_steps - 1)
            return lead + ((turn, 0) if along_rows else (0, turn))

        shape = (tile, width) if along_rows else (width, tile)
        return pl.BlockSpec((None,) * len(lead) + shape, index)

    columns = pl.BlockSpec((rows, tile), lambda i: (0, i))
    own_type = jnp.float32 if count > 1 else jnp.bfloat16
    part_types = [own_type] + [jnp.bfloat16] * (count - 1)
    weight_specs, matrices = ([], [])
    for set_no, (up_mat, up_lead, down_mat, down_lead) in enumerate(weights):
        weight_specs += [tiles(up_lead, set_no, False), tiles(down_lead, set_no, True)]
        matrices += [up_mat, down_mat]
    outs = pl.pallas_call(
        functools.partial(kernel, count, len(resident) > 0, len(weights), set_steps),
        grid=(hidden // tile,),
        in_specs=[whole(block.shape) for block in blocks]
        + [columns for _ in streamed]
        + weight_specs
        + [whole(arr.shape) for arr in resident],
        out_shape=[jax.ShapeDtypeStruct((rows, hidden), jnp.bfloat16)] * hidden_outs
        + [jax.ShapeDtypeStruct((rows, width), jnp.bfloat16)]
        + [jax.ShapeDtypeStruct((size, width), kind) for kind in part_types],
        out_specs=[columns] * hidden_outs
        + [whole((rows, width))]
        + [whole((size, width)) for _ in part_types],
        scratch_shapes=[pltpu.VMEM((rows, width), jnp.float32)],
        compiler_params=pltpu.CompilerParams(vmem_limit_bytes=40 * 2**20),
        cost_estimate=pl.CostEstimate(
            flops=4 * rows * width * hidden,
            bytes_accessed=4 * width * hidden + 6 * rows * width,
            transcendentals=2 * rows * hidden,
        ),
    )(*blocks, *streamed, *matrices, *resident)
    return outs[:hidden_outs], outs[hidden_outs], outs[hidden_outs + 1 :]


def mlp_forward(blocks, weights, moved=()):
    (act, slope), rows, parts = mlp_call(mlp_forward_kernel, blocks, (), moved, 2, weights)
    return (parts, (rows, act, slope))


def mlp_backward(blocks, slope, weights, moved=()):
    (grad_pre,), rows, parts = mlp_call(mlp_backward_kernel, blocks, (slope,), moved, 1, weights)
    return (parts, rows, grad_pre)


def norm_forward(values, gain_vec):
    center = values - jnp.mean(values, axis=-1, keepdims=True)
    scale_inv = lax.rsqrt(jnp.mean(center * center, axis=-1, keepdims=True) + epsilon)
    normal = center * scale_inv
    return (normal * gain_vec, normal, scale_inv)


def norm_backward(grad_out, normal, scale_inv, gain_vec):
    scaled = grad_out * gain_vec
    grad_values = scale_inv * (
        scaled
        - jnp.mean(scaled, axis=-1, keepdims=True)
        - normal * jnp.mean(scaled * normal, axis=-1, keepdims=True)
    )
    return (grad_values, jnp.sum(grad_out * normal, axis=0))


def is_square(axis):
    return lax.axis_size(axis) == 4


def wide_hop(value, mask):
    return lax.ppermute(value, "wide", [(i, i ^ mask) for i in range(4)])


def wide_spread(rows):
    if not is_square("wide"):
        return [lax.all_gather(rows, "wide", axis=0, tiled=True)]
    half = rows.shape[0] // 2
    y_first = wide_hop(rows[:half], 2)
    x_last = wide_hop(rows[half:], 1)
    y_last = wide_hop(rows[half:], 2)
    x_first = wide_hop(rows[:half], 1)
    d_first = wide_hop(y_first, 1)
    d_last = wide_hop(x_last, 2)
    return [
        rows,
        jnp.concatenate([x_first, x_last]),
        jnp.concatenate([y_first, y_last]),
        jnp.concatenate([d_first, d_last]),
    ]


def wide_collect(parts):
    if not is_square("wide"):
        return lax.psum_scatter(low(parts[0]), "wide", scatter_dimension=0, tiled=True).astype(
            jnp.float32
        )
    own = parts[0]
    x_part, y_part, d_low = [low(part) for part in parts[1:]]
    half = own.shape[0] // 2
    via_x = wide_hop(d_low[:half], 1)
    via_y = wide_hop(d_low[half:], 2)
    x_first = wide_hop(x_part[:half], 1)
    y_last = wide_hop(y_part[half:], 2)
    y_first = wide_hop(y_part[:half] + via_x, 2)
    x_last = wide_hop(x_part[half:] + via_y, 1)
    first = own[:half] + x_first.astype(jnp.float32) + y_first.astype(jnp.float32)
    last = own[half:] + x_last.astype(jnp.float32) + y_last.astype(jnp.float32)
    return jnp.concatenate([first, last])


def in_order(blocks):
    if len(blocks) == 1:
        return blocks[0]
    me = lax.axis_index("wide")
    stacked = jnp.stack(blocks)
    return jnp.concatenate(
        [lax.dynamic_index_in_dim(stacked, me ^ i, 0, keepdims=False) for i in range(4)]
    )


def in_blocks(values):
    if not is_square("wide"):
        return [values]
    me = lax.axis_index("wide")
    size = values.shape[0] // 4
    return [lax.dynamic_slice_in_dim(values, (me ^ i) * size, size, 0) for i in range(4)]


def expert_trade(values):
    return lax.all_to_all(values, "wide", split_axis=0, concat_axis=0, tiled=True)


def rep_hop(value, mask):
    return lax.ppermute(value, "rep", [(i, i ^ mask) for i in range(4)])


rep_pairs = [[0, 1], [2, 3]]


def rep_pair_gather(values):
    return lax.all_gather(values, "rep", axis=0, tiled=True, axis_index_groups=rep_pairs)


def rep_pair_scatter(values):
    return lax.psum_scatter(
        values, "rep", scatter_dimension=0, tiled=True, axis_index_groups=rep_pairs
    )


def rep_spread(rows):
    return [rows, rep_hop(rows, 2)]


def rep_collect(parts):
    return parts[0] + rep_hop(parts[1], 2).astype(jnp.float32)


def small_scatter(values, axis):
    if not is_square(axis):
        return lax.psum_scatter(values, axis, scatter_dimension=1, tiled=True)
    me = lax.axis_index(axis)
    size = values.shape[1] // 4

    def columns(device):
        return lax.dynamic_slice_in_dim(values, device * size, size, 1)

    total = columns(me)
    for mask in (1, 2, 3):
        pairs = [(i, i ^ mask) for i in range(4)]
        total = total + lax.ppermute(columns(me ^ mask), axis, pairs)
    return total


def joined(blocks):
    return blocks[0] if len(blocks) == 1 else jnp.concatenate(blocks)


def attention_layout(packed, segment_ids):
    row_count = packed.shape[0]
    head_count = packed.shape[1] // (3 * HD)
    seq_count = row_count // SEQ_LEN
    block_rows = min(512, SEQ_LEN)
    per_seq = SEQ_LEN // block_rows
    head_parts = packed.reshape(seq_count, SEQ_LEN, head_count, 3, HD)
    seg_table = segment_ids.reshape(seq_count, SEQ_LEN)
    return (head_parts, seg_table, block_rows, per_seq, head_count, seq_count)


def block_scores(seq_parts, seq_segs, row_start, block_rows):
    key_end = row_start + block_rows
    queries = seq_parts[row_start:key_end, :, 0]
    scores = jnp.einsum(
        "qhd,khd->hqk", queries, seq_parts[:key_end, :, 1], preferred_element_type=jnp.float32
    ) * (1.0 / math.sqrt(HD))
    seg_query = seq_segs[row_start:key_end]
    query_pos = row_start + jnp.arange(block_rows, dtype=jnp.int32)
    key_pos = jnp.arange(key_end, dtype=jnp.int32)
    allowed = (query_pos[:, None] >= key_pos[None, :]) & (
        seg_query[:, None] == seq_segs[None, :key_end]
    )
    return (jnp.where(allowed[None], scores, masked_score), queries)


def attention_forward(packed, segment_ids):
    head_parts, seg_table, block_rows, per_seq, head_count, seq_count = attention_layout(
        packed, segment_ids
    )

    def one_seq(seq_pack):
        seq_parts, seq_segs = seq_pack
        block_outs, block_logs = ([], [])
        for block_no in range(per_seq):
            row_start = block_no * block_rows
            key_end = row_start + block_rows
            scores, queries = block_scores(seq_parts, seq_segs, row_start, block_rows)
            highest = jnp.max(scores, axis=-1, keepdims=True)
            exponent = jnp.exp(scores - highest)
            row_total = jnp.sum(exponent, axis=-1, keepdims=True)
            probs_low = (exponent / row_total).astype(jnp.bfloat16)
            attended = jnp.einsum(
                "hqk,khd->qhd",
                probs_low,
                seq_parts[:key_end, :, 2],
                preferred_element_type=jnp.float32,
            )
            block_outs.append(attended.astype(jnp.bfloat16).reshape(block_rows, head_count * HD))
            block_logs.append(highest[..., 0] + jnp.log(row_total[..., 0]))
        return (jnp.concatenate(block_outs, axis=0), jnp.stack(block_logs))

    attended, log_totals = lax.map(one_seq, (head_parts, seg_table))
    return (attended.reshape(packed.shape[0], head_count * HD), log_totals)


def attention_backward(packed, segment_ids, log_totals, grad_att):
    head_parts, seg_table, block_rows, per_seq, head_count, seq_count = attention_layout(
        packed, segment_ids
    )
    grad_seqs = grad_att.reshape(seq_count, SEQ_LEN, head_count, HD)
    scale_value = 1.0 / math.sqrt(HD)

    def one_seq(seq_pack):
        seq_parts, seq_segs, seq_logs, seq_grad = seq_pack
        query_list = []
        grad_key = jnp.zeros((SEQ_LEN, head_count, HD), jnp.float32)
        grad_value = jnp.zeros((SEQ_LEN, head_count, HD), jnp.float32)
        for block_no in range(per_seq):
            row_start = block_no * block_rows
            key_end = row_start + block_rows
            scores, queries = block_scores(seq_parts, seq_segs, row_start, block_rows)
            probs = jnp.exp(scores - seq_logs[block_no][..., None])
            grad_here = seq_grad[row_start:key_end]
            grad_probs = jnp.einsum(
                "qhd,khd->hqk",
                grad_here,
                seq_parts[:key_end, :, 2],
                preferred_element_type=jnp.float32,
            )
            inner = jnp.sum(grad_probs * probs, axis=-1, keepdims=True)
            grad_scores = (probs * (grad_probs - inner)).astype(jnp.bfloat16)
            query_list.append(
                jnp.einsum(
                    "hqk,khd->qhd",
                    grad_scores,
                    seq_parts[:key_end, :, 1],
                    preferred_element_type=jnp.float32,
                )
                * scale_value
            )
            key_part = (
                jnp.einsum("hqk,qhd->khd", grad_scores, queries, preferred_element_type=jnp.float32)
                * scale_value
            )
            value_part = jnp.einsum(
                "hqk,qhd->khd",
                probs.astype(jnp.bfloat16),
                grad_here,
                preferred_element_type=jnp.float32,
            )
            pad_rows = ((0, SEQ_LEN - key_end), (0, 0), (0, 0))
            grad_key = grad_key + jnp.pad(key_part, pad_rows)
            grad_value = grad_value + jnp.pad(value_part, pad_rows)
        return (jnp.concatenate(query_list, axis=0), grad_key, grad_value)

    grad_query, grad_key, grad_value = lax.map(
        one_seq, (head_parts, seg_table, log_totals, grad_seqs)
    )
    stacked = jnp.stack([grad_query, grad_key, grad_value], axis=3)
    return stacked.reshape(packed.shape[0], head_count * 3 * HD).astype(jnp.bfloat16)


class RowOrder:
    def __init__(self, place):
        self.place = place
        self.count = place.shape[0]

    def onehot(self):
        rows = jnp.arange(self.count, dtype=jnp.int32)
        return (self.place[:, None] == rows[None, :]).astype(jnp.bfloat16)

    def to_tokens(self, rows):
        return low(matmul(self.onehot(), rows))

    def from_tokens(self, tokens):
        return low(matmul_left(self.onehot(), tokens))


def token_order(count):
    tokens = jnp.arange(count, dtype=jnp.int32)
    if not is_square("wide"):
        return RowOrder(tokens)
    return RowOrder(tokens ^ (lax.axis_index("wide") * (count // 4)))


def wide_table(values):
    if not is_square("wide"):
        return lax.all_gather(values, "wide", axis=0)
    me = lax.axis_index("wide")
    hops = jnp.stack([values] + [wide_hop(values, mask) for mask in (1, 2, 3)])
    return jnp.stack([lax.dynamic_index_in_dim(hops, me ^ i, 0, keepdims=False) for i in range(4)])


def routed_order(all_routes):
    devices, size = all_routes.shape
    experts = jnp.arange(devices, dtype=jnp.int32)
    tokens = jnp.arange(size, dtype=jnp.int32)
    same = (all_routes[:, :, None] == all_routes[:, None, :]) & (tokens[:, None] > tokens[None, :])
    rank_ids = jnp.sum(same.astype(jnp.int32), axis=2)
    owner = all_routes ^ lax.axis_index("wide") if is_square("wide") else all_routes
    place = owner * size + experts[:, None] * (size // devices) + rank_ids
    return RowOrder(place.reshape(-1))


def order_change(source, target):
    rows = jnp.arange(target.count, dtype=jnp.int32)
    found = (target.place[:, None] == rows[None, :]).astype(jnp.int32)
    return jnp.sum(found * source.place[:, None], axis=0)


def split(values):
    if not is_square("wide"):
        return [values]
    size = values.shape[0] // 4
    return [values[i * size : (i + 1) * size] for i in range(4)]


def own_start(size):
    return 0 if is_square("wide") else lax.axis_index("wide") * size


def dense_forward(block_in, segment_ids, weights, order, change):
    first_norm_gain, qkv_mat, out_mat, second_norm_gain, mlp_weights = weights
    own_size = block_in.shape[0]
    shaped_one, normal_one, inv_one = norm_forward(block_in, first_norm_gain)
    first_blocks = wide_spread(low(shaped_one))
    packed = order.to_tokens(joined([low(matmul(rows, qkv_mat)) for rows in first_blocks]))
    attended, log_totals = attention_forward(packed, segment_ids)
    attended = order.from_tokens(attended)
    middle = block_in + wide_collect([matmul(rows, out_mat) for rows in split(attended)])
    shaped_two, normal_two, inv_two = norm_forward(middle, second_norm_gain)
    second_blocks = wide_spread(low(shaped_two))
    rows = jnp.arange(change.shape[0], dtype=jnp.int32)
    moving = (change[:, None] == rows[None, :]).astype(jnp.bfloat16)
    own_rows = own_start(own_size) + jnp.arange(own_size, dtype=jnp.int32)
    own_moving = (change[:, None] == own_rows[None, :]).astype(jnp.bfloat16)
    parts, mlp_saved = mlp_forward(second_blocks, mlp_weights, (moving, own_moving, low(middle)))
    return (
        wide_collect(parts),
        (
            normal_one,
            inv_one,
            first_blocks,
            packed,
            attended,
            log_totals,
            normal_two,
            inv_two,
            mlp_saved,
            moving,
        ),
    )


def dense_backward(grad_rows, saved_state, segment_ids, weights, order, sums, last_part, finish):
    first_norm_gain, qkv_mat, out_mat, second_norm_gain, mlp_weights = weights
    (
        normal_one,
        inv_one,
        first_blocks,
        packed,
        attended,
        log_totals,
        normal_two,
        inv_two,
        (second_rows, activated, slope),
        moving,
    ) = saved_state
    own_size = grad_rows.shape[0]
    blocks, sums, last_part = together((wide_spread(grad_rows), sums, last_part))
    last_sum = rep_pair_scatter(last_part)
    parts, grad_wide, grad_pre = mlp_backward(blocks, slope, mlp_weights, (moving,))
    grad_out = lax.dynamic_slice_in_dim(grad_wide, own_start(own_size), own_size, 0)
    grad_norm_two = wide_collect(parts)
    down_part = half_summed(weight_grad([activated], [grad_wide]), 0)
    up_part = half_summed(weight_grad([second_rows], [grad_pre]), 1)
    grad_norm_two, down_part, up_part = together((grad_norm_two, down_part, up_part))
    grad_down, grad_up = rep_summed(down_part, 1), rep_summed(up_part, 0)
    grad_in_two, grad_gain_two = norm_backward(grad_norm_two, normal_two, inv_two, second_norm_gain)
    grad_middle = grad_out.astype(jnp.float32) + grad_in_two
    mid_blocks, last_sum = together((wide_spread(low(grad_middle)), last_sum))
    finished = finish([last_sum, sums])
    grad_att = order.to_tokens(joined([low(matmul_right(rows, out_mat)) for rows in mid_blocks]))
    grad_packed = attention_backward(packed, segment_ids, log_totals, grad_att)
    out_part = half_summed(low(matmul_left(attended, joined(mid_blocks))), 0)
    grad_packed, out_part, grad_down, grad_up = together(
        (grad_packed, out_part, grad_down, grad_up)
    )
    grad_packed = order.from_tokens(grad_packed)
    grad_norm_one = wide_collect([matmul_right(rows, qkv_mat) for rows in split(grad_packed)])
    qkv_part = half_summed(low(matmul_left(joined(first_blocks), grad_packed)), 1)
    grad_out_mat = rep_summed(out_part, 1)
    grad_norm_one, qkv_part, finished, grad_out_mat = together(
        (grad_norm_one, qkv_part, finished, grad_out_mat)
    )
    grad_qkv = rep_summed(qkv_part, 0)
    grad_in_one, grad_gain_one = norm_backward(grad_norm_one, normal_one, inv_one, first_norm_gain)
    return (
        grad_middle + grad_in_one,
        (grad_gain_one, grad_qkv, grad_out_mat, grad_gain_two, grad_up, grad_down),
        finished,
    )


def half_summed(partial, dim):
    section = lax.axis_index("section")
    size = partial.shape[dim] // 2
    kept = lax.dynamic_slice_in_dim(partial, section * size, size, dim)
    given = lax.dynamic_slice_in_dim(partial, (1 - section) * size, size, dim)
    return low(kept.astype(jnp.float32) + section_swap(given).astype(jnp.float32))


def rep_summed(partial, dim):
    return lax.psum_scatter(partial, "rep", scatter_dimension=dim, tiled=True)


def both_halves(layer_halves, dim):
    is_first = lax.axis_index("section") == 0
    first, second = layer_halves
    kept = jnp.where(is_first, first, second)
    moved = section_swap(jnp.where(is_first, second, first))
    parts = [jnp.where(is_first, kept, moved), jnp.where(is_first, moved, kept)]
    return jnp.concatenate(parts, axis=dim).astype(jnp.float32)


def slot_matrix_of(route_ids):
    expert_count = lax.axis_size("wide")
    capacity = max(2, route_ids.shape[0] // expert_count)
    onehot = (route_ids[:, None] == jnp.arange(expert_count, dtype=jnp.int32)[None, :]).astype(
        jnp.int32
    )
    rank_ids = jnp.sum(jnp.cumsum(onehot, axis=0) * onehot, axis=1) - 1
    position = route_ids * capacity + rank_ids
    return (
        position[:, None] == jnp.arange(expert_count * capacity, dtype=jnp.int32)[None, :]
    ).astype(jnp.bfloat16)


def weight_grad_kernel(count, *refs):
    rows, grads, out = refs[:count], refs[count:-1], refs[-1]
    total = matmul_left(rows[0][...], grads[0][...])
    for row, grad in zip(rows[1:], grads[1:]):
        total += matmul_left(row[...], grad[...])
    out[...] = low(total)


def weight_grad(rows, grads, rows_half=None, columns_half=None):
    height, width = rows[0].shape[1], grads[0].shape[1]
    if rows_half is not None:
        height = height // 2
    if columns_half is not None:
        width = width // 2
    tile = hidden_tile(height)
    first, column = (rows_half or 0) * (height // tile), columns_half or 0
    depth = sum(arr.shape[0] for arr in rows)
    return pl.pallas_call(
        functools.partial(weight_grad_kernel, len(rows)),
        grid=(height // tile,),
        in_specs=[pl.BlockSpec((arr.shape[0], tile), lambda i: (0, i + first)) for arr in rows]
        + [pl.BlockSpec((arr.shape[0], width), lambda i: (0, column)) for arr in grads],
        out_shape=jax.ShapeDtypeStruct((height, width), jnp.bfloat16),
        out_specs=pl.BlockSpec((tile, width), lambda i: (i, 0)),
        compiler_params=pltpu.CompilerParams(vmem_limit_bytes=24 * 2**20),
        cost_estimate=pl.CostEstimate(
            flops=2 * depth * height * width,
            bytes_accessed=2 * (depth * (height + width) + height * width),
            transcendentals=0,
        ),
    )(*rows, *grads)


def chunked(values):
    half = values.shape[0] // 2
    return [values[:half], values[half:]]


def expert_forward(rows_in, centroid, gain_rows, mlp_weights):
    hidden, saved = ([], [])
    starts = [low(rows) for rows in chunked(rows_in)]
    states = [rows.astype(jnp.float32) for rows in starts]
    sublayer_saved = []
    for sublayer in range(2):
        kept = []
        for i, current in enumerate(states):
            shaped, normal, scale_inv = norm_forward(current, gain_rows[sublayer])
            shaped = low(shaped)
            blocks = rep_spread(shaped)
            parts, mlp_saved = mlp_forward(blocks, mlp_weights(sublayer))
            kept.append((normal, scale_inv, mlp_saved))
            states[i] = current + rep_collect(parts)
        sublayer_saved.append(kept)
    for arrived, current in zip(starts, states):
        starting_rows = arrived.astype(jnp.float32)
        gate_value = jax.nn.sigmoid(jnp.dot(arrived, centroid, preferred_element_type=jnp.float32))
        gate = gate_value[:, None]
        hidden.append(low(gate * current + (1.0 - gate) * starting_rows))
        saved.append((arrived, gate_value, current))
    return (jnp.concatenate(hidden), (saved, sublayer_saved))


def expert_backward(grad_rows, saved_state, centroid, gain_rows, mlp_weights, mid):
    saved, sublayer_saved = saved_state
    states, start_grads = ([], [])
    grad_centroid = jnp.zeros(centroid.shape, jnp.float32)
    for rows, (arrived, gate_value, final_state) in zip(chunked(grad_rows), saved):
        starting_rows = arrived.astype(jnp.float32)
        grad_mixed = rows.astype(jnp.float32)
        grad_gate = jnp.sum(grad_mixed * (final_state - starting_rows), axis=-1)
        grad_logit = grad_gate * gate_value * (1.0 - gate_value)
        grad_centroid += jnp.dot(grad_logit, starting_rows, precision=highest_prec)
        states.append(gate_value[:, None] * grad_mixed)
        start_grads.append(
            (1.0 - gate_value[:, None]) * grad_mixed
            + grad_logit[:, None] * centroid.astype(jnp.float32)[None, :]
        )
    gain_list, weight_grads = ([], [])
    for sublayer in (1, 0):
        collected, pieces = ([], [])
        for i, (_, _, (rows, act, slope)) in enumerate(sublayer_saved[sublayer]):
            given = low(states[i])
            blocks = rep_spread(given)
            parts, grad_wide, grad_pre = mlp_backward(blocks, slope, mlp_weights(sublayer))
            collected.append(rep_collect(parts))
            pieces.append((act, grad_wide, rows, grad_pre))
        if sublayer == 0:
            collected[0], weight_grads, mid = together((collected[0], weight_grads, mid))
            weight_grads = [rep_pair_scatter(part) for part in weight_grads]
        acts, grads_wide, rows, grads_pre = zip(*pieces)
        weight_grads.append(pair_weight_grads(rows, grads_pre, acts, grads_wide))
        gain = 0.0
        for i, (normal, scale_inv, _) in enumerate(sublayer_saved[sublayer]):
            grad_values, grad_gain = norm_backward(
                collected[i], normal, scale_inv, gain_rows[sublayer]
            )
            gain += grad_gain
            states[i] = states[i] + grad_values
        gain_list.append(gain)
    grad_start = jnp.concatenate([low(a + b) for a, b in zip(start_grads, states)])
    return (grad_start, (grad_centroid, gain_list[::-1]), weight_grads[::-1], mid)


def pair_weight_kernel(count, prefetched, *refs):
    rows, grads_pre, acts, grads_wide = [refs[i * count : (i + 1) * count] for i in range(4)]
    kept, given = refs[4 * count :]
    which = pl.program_id(0) ^ prefetched[0]

    def write(lefts, rights):
        total = matmul_left(lefts[0][...], rights[0][...])
        for left, right in zip(lefts[1:], rights[1:]):
            total += matmul_left(left[...], right[...])

        @pl.when(pl.program_id(0) == 0)
        def _():
            kept[...] = low(total)

        @pl.when(pl.program_id(0) == 1)
        def _():
            given[...] = low(total)

    @pl.when(which == 0)
    def _():
        write(rows, grads_pre)

    @pl.when(which == 1)
    def _():
        write(acts, grads_wide)


def pair_weight_grads(rows, grads_pre, acts, grads_wide):
    count, width = len(rows), rows[0].shape[1]
    tile = hidden_tile(width)
    tiles = width // tile
    last = tiles - 1

    def which(slot, fetched):
        return slot ^ fetched[0]

    def columns(arr, index):
        return pl.BlockSpec((arr.shape[0], tile), index)

    def row_index(slot, member, i, fetched):
        return (0, jnp.where(which(slot, fetched) == 0, i, 0))

    def pre_index(slot, member, i, fetched):
        return (0, jnp.where(which(slot, fetched) == 0, member, 0))

    def act_index(slot, member, i, fetched):
        return (0, jnp.where(which(slot, fetched) == 1, member * tiles + i, 0))

    def kept_index(slot, member, i, fetched):
        return (jnp.where(slot == 0, member, 1), jnp.where(slot == 0, i, last), 0)

    def given_index(slot, member, i, fetched):
        return (jnp.where(slot == 1, member, 0), jnp.where(slot == 1, i, 0), 0)

    depth = sum(arr.shape[0] for arr in rows)
    kept, given = pl.pallas_call(
        functools.partial(pair_weight_kernel, count),
        out_shape=[jax.ShapeDtypeStruct((2, width, width), jnp.bfloat16)] * 2,
        grid_spec=pltpu.PrefetchScalarGridSpec(
            num_scalar_prefetch=1,
            grid=(2, 2, tiles),
            in_specs=[columns(arr, row_index) for arr in rows]
            + [pl.BlockSpec((arr.shape[0], width), pre_index) for arr in grads_pre]
            + [columns(arr, act_index) for arr in acts]
            + [pl.BlockSpec(arr.shape, lambda s, m, i, f: (0, 0)) for arr in grads_wide],
            out_specs=[
                pl.BlockSpec((None, tile, width), kept_index),
                pl.BlockSpec((None, tile, width), given_index),
            ],
        ),
        compiler_params=pltpu.CompilerParams(vmem_limit_bytes=32 * 2**20),
        cost_estimate=pl.CostEstimate(
            flops=8 * depth * width * width,
            bytes_accessed=8 * width * width + 16 * depth * width,
            transcendentals=0,
        ),
    )(lax.axis_index("section").reshape(1), *rows, *grads_pre, *acts, *grads_wide)
    return low(kept.astype(jnp.float32) + section_swap(given).astype(jnp.float32))


def own_layer_kernel(fetched, zero_first, zero_second, one_first, one_second, moved, up, down):
    section = fetched[0]
    sums = ((zero_first, zero_second), (one_first, one_second))
    for layer in range(2):
        for k in range(2):

            @pl.when((section == layer) & (pl.program_id(0) == k))
            def _(layer=layer, k=k):
                mine, other = ((up, down), (down, up))[layer]
                mine[...] = sums[layer][k][...].astype(jnp.float32)
                other[...] = moved[...].astype(jnp.float32)


def own_layer_grads(zero_sums, one_sums):
    section = lax.axis_index("section")
    zero, one = [[arr[0] for arr in sums] for sums in (zero_sums, one_sums)]
    given = [jnp.where(section == 0, one[k], zero[k]) for k in range(2)]
    moved = section_swap(jnp.stack(given))
    height, width = zero[0].shape
    tile = height // 4

    def block_of(layer, number):
        def index(k, i, fetched):
            chosen = (fetched[0] == layer) & (k == number)
            return (jnp.where(chosen, i, 0), 0)

        return pl.BlockSpec((tile, width), index)

    stacked = pl.BlockSpec((None, tile, width), lambda k, i, fetched: (k, i, 0))
    return pl.pallas_call(
        own_layer_kernel,
        out_shape=[jax.ShapeDtypeStruct((2, height, width), jnp.float32)] * 2,
        grid_spec=pltpu.PrefetchScalarGridSpec(
            num_scalar_prefetch=1,
            grid=(2, height // tile),
            in_specs=[block_of(layer, k) for layer in range(2) for k in range(2)] + [stacked],
            out_specs=[stacked, stacked],
        ),
        compiler_params=pltpu.CompilerParams(vmem_limit_bytes=32 * 2**20),
    )(section.reshape(1), *zero, *one, moved)


def shards(
    tokens_in,
    cotangent,
    segments,
    routes,
    ln1_gain,
    w_qkv,
    w_out,
    ln2_gain,
    w_up,
    w_down,
    centroids,
    sub_gains,
    expert_up,
    expert_down,
):
    section = lax.axis_index("section")
    is_first = section == 0

    def mine(table):
        return lax.dynamic_index_in_dim(table, section, 0, keepdims=False)

    def theirs(table):
        return lax.dynamic_index_in_dim(table, 1 - section, 0, keepdims=False)

    def both_layers(own):
        other = section_swap(own)
        return (jnp.where(is_first, own, other), jnp.where(is_first, other, own))

    route_table = routes[0, :, :, 0]
    own_routes = mine(route_table)
    other_routes = section_swap(theirs(route_table))
    layer_routes = jnp.stack(
        [jnp.where(is_first, own_routes, other_routes), jnp.where(is_first, other_routes, own_routes)]
    )
    route_tables = wide_table(layer_routes)
    plane_rows = route_table.shape[1] * lax.axis_size("wide")
    orders = [token_order(plane_rows)] + [routed_order(route_tables[:, i]) for i in range(2)]
    changes = [order_change(orders[i], orders[i + 1]) for i in range(2)]

    def stacked_layers(own):
        return lax.all_gather(own, "section", axis=0, tiled=True)

    ln1_pair, ln2_pair = both_layers(ln1_gain[0]), both_layers(ln2_gain[0])
    qkv_pair, out_pair = both_layers(w_qkv[0]), both_layers(w_out[0])
    up_pair, down_pair = both_layers(w_up[0]), both_layers(w_down[0])
    center_pair, gain_pair = both_layers(centroids[0, 0]), both_layers(sub_gains[0, 0])
    def split_layer(layer):
        if layer == 0:
            piece = jnp.where(is_first, expert_ups, section_send(expert_downs, 0))
        else:
            piece = jnp.where(is_first, section_send(expert_ups, 1), expert_downs)
        return rep_pair_gather(piece[None])

    segment_ids = mine(segments)
    hidden = mine(tokens_in)
    expert_ups, expert_downs = after((expert_up[0, 0], expert_down[0, 0]), hidden)
    gathered = split_layer(0)
    layer_matrices = [None, None]
    second_inputs = (expert_ups, expert_downs)

    dense_weights = []
    for i in range(2):
        dense_weights.append(
            (
                ln1_pair[i],
                qkv_pair[i],
                out_pair[i],
                ln2_pair[i],
                [(up_pair[i], (), down_pair[i], ())],
            )
        )

    def expert_weights(layer):
        def sublayer_weights(k):
            mats = layer_matrices[layer]
            return [(mats, (0, i, k), mats, (1, i, k)) for i in range(2)]

        return (center_pair[layer], gain_pair[layer], sublayer_weights)

    slot_matrix = slot_matrix_of(layer_routes[1])
    grad = expert_trade(low(matmul_left(slot_matrix, mine(cotangent))))
    saved = []
    for layer in range(2):
        rows_in, dense_saved = dense_forward(
            hidden.astype(jnp.float32),
            segment_ids,
            dense_weights[layer],
            orders[layer],
            changes[layer],
        )
        layer_matrices[layer] = stacked_layers(after(gathered, dense_saved[-2][0])[None])
        if layer == 0:
            expert_ups, expert_downs = after(second_inputs, rows_in)
            gathered = split_layer(1)
        hidden, expert_saved = expert_forward(rows_in, *expert_weights(layer))
        saved.append((dense_saved, expert_saved))
    produced = low(matmul(slot_matrix, expert_trade(hidden)))

    grad, expert_one, parts, _ = expert_backward(low(grad), saved[1][1], *expert_weights(1), ())
    grad, dense_one, sums_one = dense_backward(
        grad, saved[1][0], segment_ids, dense_weights[1], orders[1], parts[1], parts[0], list
    )
    grad, expert_zero, parts, dense_one = expert_backward(
        low(grad), saved[0][1], *expert_weights(0), dense_one
    )
    grad, dense_zero, (expert_up_grad, expert_down_grad) = dense_backward(
        grad,
        saved[0][0],
        segment_ids,
        dense_weights[0],
        orders[0],
        parts[1],
        parts[0],
        lambda sums_zero: own_layer_grads(sums_zero, sums_one),
    )
    grads = [(dense_zero, expert_zero), (dense_one, expert_one)]

    half_width = produced.shape[1] // 2

    def halves_out(value):
        given = lax.dynamic_slice_in_dim(value, (1 - section) * half_width, half_width, 1)
        kept = lax.dynamic_slice_in_dim(value, section * half_width, half_width, 1)
        moved = section_swap(low(given)).astype(value.dtype)
        return jnp.stack([jnp.where(is_first, kept, moved), jnp.where(is_first, moved, kept)])

    block_out = halves_out(produced)
    grad_input = halves_out(grad)

    dense_pairs = list(zip(grads[0][0], grads[1][0]))
    gains_one, qkv_pair, out_pair, gains_two, up_pair, down_pair = dense_pairs
    gain_rows = jnp.stack([gains_one[0], gains_two[0], gains_one[1], gains_two[1]])
    gain_rows = gain_rows + section_swap(gain_rows)
    gain_rows = mine(gain_rows.reshape(2, 2, -1))
    gain_sums = small_scatter(small_scatter(gain_rows, "wide"), "rep")

    def own_sum(pair):
        first = pair[0].astype(jnp.float32) + section_send(low(pair[0]), 1).astype(jnp.float32)
        second = pair[1].astype(jnp.float32) + section_send(low(pair[1]), 0).astype(jnp.float32)
        return jnp.where(is_first, first, second)

    small = [jnp.concatenate([g[1][0][None]] + [v[None] for v in g[1][1]]) for g in grads]
    small_sum = small_scatter(own_sum(small), "rep")
    return (
        block_out,
        grad_input,
        gain_sums[0][None],
        both_halves(qkv_pair, 1)[None],
        both_halves(out_pair, 0)[None],
        gain_sums[1][None],
        both_halves(up_pair, 1)[None],
        both_halves(down_pair, 0)[None],
        small_sum[0][None, None],
        small_sum[1:][None, None],
        expert_up_grad[None, None],
        expert_down_grad[None, None],
    )


def solution(mesh):
    in_specs = (
        P(None, ("rep", "wide"), None),
        P(None, ("rep", "wide"), None),
        P(None, "rep"),
        P("section", None, ("rep", "wide"), None),
        P("section", None),
        P("section", None, "wide"),
        P("section", "wide", None),
        P("section", None),
        P("section", None, "wide"),
        P("section", "wide", None),
        P("section", "wide", None),
        P("section", "wide", None, None),
        P("section", "wide", None, None, "rep"),
        P("section", "wide", None, "rep", None),
    )
    out_specs = (
        P(None, ("rep", "wide"), "section"),
        P(None, ("rep", "wide"), "section"),
        P("section", ("wide", "rep")),
        P("section", "rep", "wide"),
        P("section", "wide", "rep"),
        P("section", ("wide", "rep")),
        P("section", "rep", "wide"),
        P("section", "wide", "rep"),
        P("section", "wide", "rep"),
        P("section", "wide", None, "rep"),
        P("section", "wide", None, None, "rep"),
        P("section", "wide", None, "rep", None),
    )
    return jax.shard_map(shards, mesh=mesh, in_specs=in_specs, out_specs=out_specs, check_vma=False)
```

time: 2930 us -> 1300 us (0.44)
  waiting for transfers between devices: 1980 us -> 536 us
  matrix products: 458 us -> 83.8 us
  Pallas kernels: 0 us -> 212 us
  starting transfers between devices: 16.2 us -> 178 us
  blocking collectives: 116 us -> 0 us
  other arithmetic: 271 us -> 167 us
    reduce_scatter x28 -> x12, waiting for transfers between devices: 1030 us -> 6.52 us  [the longest x8 6.52 us: rep_summed(): return lax.psum_scatter(partial, 'rep', scatter_dimension=dim, tiled=True)]
    all_gather x24 -> x4, waiting for transfers between devices: 842 us -> 28.3 us  [the longest x2 28.3 us: rep_pair_gather(): lax.all_gather(values, 'rep', axis=0, tiled=True, axis_index_groups=rep_p...]
    ppermute x5 -> x173, waiting for transfers between devices: 7.61 us -> 494 us  [the longest x32 297 us: rep_hop(): return lax.ppermute(value, 'rep', [(i, i ^ mask) for i in range(4)])]
    pallas_call x0 -> x29, Pallas kernels: none -> 212 us  [the longest x20 159 us: mlp_call(): pl.pallas_call(functools.partial(kernel, count, len(resident) > 0, len(we...]
    ppermute x5 -> x173, starting transfers between devices: 0.15 us -> 168 us  [the longest x99 113 us: wide_hop(): return lax.ppermute(value, 'wide', [(i, i ^ mask) for i in range(4)])]
    dot_general x30 -> x9, matrix products: 132 us -> 20.1 us  [matmul_left(): lax.dot_general(first_arg, second_arg, (((0,), (0,)), ((), ())), preferre...]
    all_to_all x9 -> x0, blocking collectives: 104 us -> none  [expert_trade(): lax.all_to_all(values, 'wide', split_axis=0, concat_axis=0, tiled=True)]
    dot_general x30 -> x21, matrix products: 120 us -> 16.5 us  [matmul(): return jnp.dot(first_arg, second_arg, preferred_element_type=jnp.float32)]
  transfers between devices with their start and end apart: 62 -> 191, of which waited for: 55 -> 92; matrix products, arithmetic and copies ran while one was open for 13% -> 20% of each run, Pallas kernels for 0% -> 14%
where the time goes in v1:
time: 1300 us; the launch traced here: 1280 us
  waiting for transfers between devices  536 us (41%)
  Pallas kernels  212 us (16%)
  starting transfers between devices  178 us (14%)
  other arithmetic  167 us (13%)
  local copies, waits for them, and re-layouts  87.4 us (7%)
  matrix products  83.8 us (6%)
  between operations  19.6 us (2%)
    ppermute x32, waiting for transfers between devices, rep_hop(): return lax.ppermute(value, 'rep', [(i, i ^ mask) for i in range(4)])  297 us
    ppermute x99, waiting for transfers between devices, wide_hop(): return lax.ppermute(value, 'wide', [(i, i ^ mask) for i in range(4)])  189 us
    pallas_call x20, Pallas kernels, mlp_call(): pl.pallas_call(functools.partial(kernel, count, len(resident) > 0, len(we...  159 us
    ppermute x99, starting transfers between devices, wide_hop(): return lax.ppermute(value, 'wide', [(i, i ^ mask) for i in range(4)])  113 us
    unnamed x660, local copies, waits for them, and re-layouts  66.5 us
    convert_element_type x35, other arithmetic, low(): return value.astype(jnp.bfloat16)  51.7 us
    ppermute x32, starting transfers between devices, rep_hop(): return lax.ppermute(value, 'rep', [(i, i ^ mask) for i in range(4)])  34.4 us
    pallas_call x4, Pallas kernels, pair_weight_grads(): pl.pallas_call(functools.partial(pair_weight_kernel, count), out_shape=[j...  33.5 us
  transfers between devices with their start and end apart: 191, of which 92 were waited for; matrix products, arithmetic and copies ran while one was open for 20% of the time, Pallas kernels for 14%

profile of v1, /device:TPU:0, one launch (start us, length us, event | category | flops | bytes accessed | tf_op | source)
XLA Modules:
  0.0 1283.7 jit_solution(15866169539918793286)
XLA Ops:
  126.9 12.3 shard_map.229
  144.8 28.3 %all-gather.9.cloned.1.call-done = bf16[4,1024,1024]{2,1,0:T(8,128)(2,1)} async-done(((bf16[2,1024,1024]{2,1,0:T(8,128)(2,1)}), bf16[4,1024,1024]{2,1,0:T(8,128)(2,1)}) %all-gather.9.cloned.1.call-update) | async-done | bytes 8388624 | tf_op jit(solution)/shard_map/all_gather | solution.py:314
  202.3 14.9 %collective-permute-done.41.refs_1_ = bf16[128,1024]{1,0:T(8,128)(2,1)S(1)} collective-permute-done((bf16[128,1024]{1,0:T(8,128)(2,1)S(1)}, bf16[128,1024]{1,0:T(8,128)(2,1)S(1)}, u32[]{:S(2)}, u32[]{:S(2)}) %collective-permute-start.41) | collective-permute-done | bytes 262176 | tf_op jit(solution)/shard_map/ppermute | solution.py:307
  255.6 16.1 %collective-permute-done.43.refs_1_ = bf16[128,1024]{1,0:T(8,128)(2,1)S(1)} collective-permute-done((bf16[128,1024]{1,0:T(8,128)(2,1)S(1)}, bf16[128,1024]{1,0:T(8,128)(2,1)S(1)}, u32[]{:S(2)}, u32[]{:S(2)}) %collective-permute-start.43) | collective-permute-done | bytes 262176 | tf_op jit(solution)/shard_map/ppermute | solution.py:307
  298.9 8.8 collective-permute-done.37
  392.7 12.3 shard_map.234
  446.7 15.5 %collective-permute-done.66.refs_1_ = bf16[128,1024]{1,0:T(8,128)(2,1)S(1)} collective-permute-done((bf16[128,1024]{1,0:T(8,128)(2,1)S(1)}, bf16[128,1024]{1,0:T(8,128)(2,1)S(1)}, u32[]{:S(2)}, u32[]{:S(2)}) %collective-permute-start.66) | collective-permute-done | bytes 262176 | tf_op jit(solution)/shard_map/ppermute | solution.py:307
  489.7 10.4 collective-permute-done.75
  536.7 13.7 %collective-permute-done.76.refs_1_ = bf16[128,1024]{1,0:T(8,128)(2,1)S(1)} collective-permute-done((bf16[128,1024]{1,0:T(8,128)(2,1)S(1)}, bf16[128,1024]{1,0:T(8,128)(2,1)S(1)}, u32[]{:S(2)}, u32[]{:S(2)}) %collective-permute-start.76) | collective-permute-done | bytes 262176 | tf_op jit(solution)/shard_map/ppermute | solution.py:307
  572.8 14.7 %collective-permute-done.81.refs_1_ = bf16[128,1024]{1,0:T(8,128)(2,1)S(1)} collective-permute-done((bf16[128,1024]{1,0:T(8,128)(2,1)S(1)}, bf16[128,1024]{1,0:T(8,128)(2,1)S(1)}, u32[]{:S(2)}, u32[]{:S(2)}) %collective-permute-start.81) | collective-permute-done | bytes 262176 | tf_op jit(solution)/shard_map/ppermute | solution.py:307
  595.0 13.8 %collective-permute-done.82 = bf16[128,1024]{1,0:T(8,128)(2,1)S(1)} collective-permute-done((bf16[128,1024]{1,0:T(8,128)(2,1)S(1)}, bf16[128,1024]{1,0:T(8,128)(2,1)S(1)}, u32[]{:S(2)}, u32[]{:S(2)}) %collective-permute-start.82) | collective-permute-done | bytes 262176 | tf_op jit(solution)/shard_map/ppermute | solution.py:307
  616.9 17.1 %collective-permute-done.77 = bf16[128,1024]{1,0:T(8,128)(2,1)S(1)} collective-permute-done((bf16[128,1024]{1,0:T(8,128)(2,1)S(1)}, bf16[128,1024]{1,0:T(8,128)(2,1)S(1)}, u32[]{:S(2)}, u32[]{:S(2)}) %collective-permute-start.77) | collective-permute-done | bytes 262176 | tf_op jit(solution)/shard_map/ppermute | solution.py:307
  642.9 14.3 %collective-permute-done.86.refs_1_ = bf16[128,1024]{1,0:T(8,128)(2,1)S(1)} collective-permute-done((bf16[128,1024]{1,0:T(8,128)(2,1)S(1)}, bf16[128,1024]{1,0:T(8,128)(2,1)S(1)}, u32[]{:S(2)}, u32[]{:S(2)}) %collective-permute-start.86) | collective-permute-done | bytes 262176 | tf_op jit(solution)/shard_map/ppermute | solution.py:307
  675.2 12.6 collective-permute-done.87
  727.5 10.8 shard_map.245
  873.0 14.3 %collective-permute-done.121.refs_1_ = bf16[128,1024]{1,0:T(8,128)(2,1)S(1)} collective-permute-done((bf16[128,1024]{1,0:T(8,128)(2,1)S(1)}, bf16[128,1024]{1,0:T(8,128)(2,1)S(1)}, u32[]{:S(2)}, u32[]{:S(2)}) %collective-permute-start.121) | collective-permute-done | bytes 262176 | tf_op jit(solution)/shard_map/ppermute | solution.py:307
  901.8 9.1 shard_map.251
  916.0 30.0 %collective-permute-done.123 = bf16[128,1024]{1,0:T(8,128)(2,1)} collective-permute-done((bf16[128,1024]{1,0:T(8,128)(2,1)S(1)}, bf16[128,1024]{1,0:T(8,128)(2,1)}, u32[]{:S(2)}, u32[]{:S(2)}) %collective-permute-start.123) | collective-permute-done | bytes 262176 | tf_op jit(solution)/shard_map/ppermute | solution.py:307
  957.6 13.3 %collective-permute-done.119.refs_1_ = bf16[128,1024]{1,0:T(8,128)(2,1)S(1)} collective-permute-done((bf16[128,1024]{1,0:T(8,128)(2,1)S(1)}, bf16[128,1024]{1,0:T(8,128)(2,1)S(1)}, u32[]{:S(2)}, u32[]{:S(2)}) %collective-permute-start.119) | collective-permute-done | bytes 262176 | tf_op jit(solution)/shard_map/ppermute | solution.py:307
  978.6 14.4 %collective-permute-done.120 = bf16[128,1024]{1,0:T(8,128)(2,1)S(1)} collective-permute-done((bf16[128,1024]{1,0:T(8,128)(2,1)S(1)}, bf16[128,1024]{1,0:T(8,128)(2,1)S(1)}, u32[]{:S(2)}, u32[]{:S(2)}) %collective-permute-start.120) | collective-permute-done | bytes 262176 | tf_op jit(solution)/shard_map/ppermute | solution.py:307
  1000.6 13.7 %collective-permute-done.124.refs_1_ = bf16[128,1024]{1,0:T(8,128)(2,1)S(1)} collective-permute-done((bf16[128,1024]{1,0:T(8,128)(2,1)S(1)}, bf16[128,1024]{1,0:T(8,128)(2,1)S(1)}, u32[]{:S(2)}, u32[]{:S(2)}) %collective-permute-start.124) | collective-permute-done | bytes 262176 | tf_op jit(solution)/shard_map/ppermute | solution.py:307
  1030.1 14.7 %collective-permute-done.125 = bf16[128,1024]{1,0:T(8,128)(2,1)S(1)} collective-permute-done((bf16[128,1024]{1,0:T(8,128)(2,1)S(1)}, bf16[128,1024]{1,0:T(8,128)(2,1)S(1)}, u32[]{:S(2)}, u32[]{:S(2)}) %collective-permute-start.125) | collective-permute-done | bytes 262176 | tf_op jit(solution)/shard_map/ppermute | solution.py:307
  1098.7 10.6 shard_map.254
  1242.5 9.0 shard_map.257
  (1449 shorter events, 919.3 us)
Async XLA Ops:
  7.2 165.9 %all-gather.9.cloned.1.call-start = ((), (), s32[]{:S(2)}) async-start(), calls=%async_computation.26 | async-start | bytes 12582912 | tf_op jit(solution)/shard_map/all_gather | solution.py:314
  22.4 43.4 %collective-permute-start.34 = (bf16[2,1024,1024]{2,1,0:T(8,128)(2,1)}, bf16[2,1024,1024]{2,1,0:T(8,128)(2,1)S(1)}, u32[]{:S(2)}, u32[]{:S(2)}) collective-permute-start(bf16[2,1024,1024]{2,1,0:T(8,128)(2,1)} %bitcast.542), channel_id=1, source_target_pairs={{0,16},{1,17},{2,18},{3,19},{4,20},{5,21},{6,22},{7,23},{8,24},{9,... | collective-permute-start | bytes 12582920 | tf_op jit(solution)/shard_map/ppermute | solution.py:27
  29.7 79.7 %collective-permute-start.24 = (bf16[1024,1024]{1,0:T(8,128)(2,1)}, bf16[1024,1024]{1,0:T(8,128)(2,1)}, u32[]{:S(2)}, u32[]{:S(2)}) collective-permute-start(bf16[1024,1024]{1,0:T(8,128)(2,1)} %bitcast.25), channel_id=1, source_target_pairs={{0,16},{16,0},{1,17},{17,1},{2,18},{18,2},{3,19},{19,3},{4,20},{20... | collective-permute-start | bytes 6291464 | tf_op jit(solution)/shard_map/ppermute | solution.py:23
  69.5 148.4 %all-gather.11.cloned.1.call-start = ((), (), s32[]{:S(2)}) async-start(), calls=%async_computation.27 | async-start | bytes 25165824 | tf_op jit(solution)/shard_map/all_gather | solution.py:906
  173.1 238.4 %all-gather.13.cloned.1.call-start = ((), (), s32[]{:S(2)}) async-start(), calls=%async_computation.28 | async-start | bytes 12582912 | tf_op jit(solution)/shard_map/all_gather | solution.py:314
  177.3 105.1 %collective-permute-start.67 = (bf16[2,1024,1024]{2,1,0:T(8,128)(2,1)}, bf16[2,1024,1024]{2,1,0:T(8,128)(2,1)}, u32[]{:S(2)}, u32[]{:S(2)}) collective-permute-start(bf16[2,1024,1024]{2,1,0:T(8,128)(2,1)} %bitcast.540), channel_id=1, source_target_pairs={{16,0},{17,1},{18,2},{19,3},{20,4},{21,5},{22,6},{23,7},{24,8},{25... | collective-permute-start | bytes 12582920 | tf_op jit(solution)/shard_map/ppermute | solution.py:27
  287.3 175.0 %all-gather.15.cloned.1.call-start = ((), (), s32[]{:S(2)}) async-start(), calls=%async_computation.29 | async-start | bytes 25165824 | tf_op jit(solution)/shard_map/all_gather | solution.py:906
  421.6 298.4 %reduce-scatter.13.cloned.1.call-start = ((), (), s32[]{:S(2)}) async-start(), calls=%async_computation.14 | async-start | bytes 6291456 | tf_op jit(solution)/shard_map/reduce_scatter | solution.py:318
  471.5 38.6 %collective-permute-start.79 = (bf16[128,1024]{1,0:T(8,128)(2,1)S(1)}, bf16[128,1024]{1,0:T(8,128)(2,1)S(1)}, u32[]{:S(2)}, u32[]{:S(2)}) collective-permute-start(bf16[128,1024]{1,0:T(8,128)(2,1)S(1)} %fusion.204.refs_0_), channel_id=1, source_target_pairs={{0,2},{1,3},{2,0},{3,1},{4,6},{5,7},{6,4},{7,5},{8,10},{9,11},{10,... | collective-permute-start | bytes 786440 | tf_op jit(solution)/shard_map/ppermute | solution.py:307
  613.9 191.8 %reduce-scatter.15.cloned.1.call-start = ((), (), s32[]{:S(2)}) async-start(), calls=%async_computation.15 | async-start | bytes 6291456 | tf_op jit(solution)/shard_map/reduce_scatter | solution.py:318
  672.3 43.5 %collective-permute-start.94 = (bf16[2,1024,1024]{2,1,0:T(8,128)(2,1)S(1)}, bf16[2,1024,1024]{2,1,0:T(8,128)(2,1)S(1)}, u32[]{:S(2)}, u32[]{:S(2)}) collective-permute-start(bf16[2,1024,1024]{2,1,0:T(8,128)(2,1)S(1)} %get-tuple-element.325), channel_id=1, source_target_pairs={{0,16},{16,0},{1,17},{17,1},{2,18},{18,2},{3,19},{19,3},{4,20},{20... | collective-permute-start | bytes 12582920 | tf_op jit(solution)/shard_map/ppermute | solution.py:23
  720.0 107.6 %reduce-scatter.17.cloned.1.call-start = ((), (), s32[]{:S(2)}) async-start(), calls=%async_computation.16 | async-start | bytes 1310720 | tf_op jit(solution)/shard_map/reduce_scatter | solution.py:615
  776.3 54.5 %reduce-scatter.19.cloned.1.call-start = ((), (), s32[]{:S(2)}) async-start(), calls=%async_computation.17 | async-start | bytes 1310720 | tf_op jit(solution)/shard_map/reduce_scatter | solution.py:615
  798.5 68.3 %reduce-scatter.21.cloned.1.call-start = ((), (), s32[]{:S(2)}) async-start(), calls=%async_computation.18 | async-start | bytes 327680 | tf_op jit(solution)/shard_map/reduce_scatter | solution.py:615
  843.9 156.3 %reduce-scatter.23.cloned.1.call-start = ((), (), s32[]{:S(2)}) async-start(), calls=%async_computation.19 | async-start | bytes 983040 | tf_op jit(solution)/shard_map/reduce_scatter | solution.py:615
  913.0 80.9 %collective-permute-start.122 = (bf16[2,1024,1024]{2,1,0:T(8,128)(2,1)}, bf16[2,1024,1024]{2,1,0:T(8,128)(2,1)}, u32[]{:S(2)}, u32[]{:S(2)}) collective-permute-start(bf16[2,1024,1024]{2,1,0:T(8,128)(2,1)} %get-tuple-element.367), channel_id=1, source_target_pairs={{0,16},{16,0},{1,17},{17,1},{2,18},{18,2},{3,19},{19,3},{4,20},{20... | collective-permute-start | bytes 12582920 | tf_op jit(solution)/shard_map/ppermute | solution.py:23
  913.0 39.2 %collective-permute-start.118 = (bf16[128,1024]{1,0:T(8,128)(2,1)}, bf16[128,1024]{1,0:T(8,128)(2,1)}, u32[]{:S(2)}, u32[]{:S(2)}) collective-permute-start(bf16[128,1024]{1,0:T(8,128)(2,1)} %get-tuple-element.353), channel_id=1, source_target_pairs={{0,2},{1,3},{2,0},{3,1},{4,6},{5,7},{6,4},{7,5},{8,10},{9,11},{10,... | collective-permute-start | bytes 786440 | tf_op jit(solution)/shard_map/ppermute | solution.py:307
  915.9 154.6 %reduce-scatter.25.cloned.1.call-start = ((), (), s32[]{:S(2)}) async-start(), calls=%async_computation.20 | async-start | bytes 6291456 | tf_op jit(solution)/shard_map/reduce_scatter | solution.py:318
  1000.3 170.2 %reduce-scatter.27.cloned.1.call-start = ((), (), s32[]{:S(2)}) async-start(), calls=%async_computation.21 | async-start | bytes 6291456 | tf_op jit(solution)/shard_map/reduce_scatter | solution.py:318
  1083.0 115.1 %reduce-scatter.29.cloned.1.call-start = ((), (), s32[]{:S(2)}) async-start(), calls=%async_computation.22 | async-start | bytes 1310720 | tf_op jit(solution)/shard_map/reduce_scatter | solution.py:615
  1142.0 56.1 %reduce-scatter.31.cloned.1.call-start = ((), (), s32[]{:S(2)}) async-start(), calls=%async_computation.23 | async-start | bytes 1310720 | tf_op jit(solution)/shard_map/reduce_scatter | solution.py:615
  1161.6 89.9 %reduce-scatter.33.cloned.1.call-start = ((), (), s32[]{:S(2)}) async-start(), calls=%async_computation.24 | async-start | bytes 327680 | tf_op jit(solution)/shard_map/reduce_scatter | solution.py:615
  1185.5 52.2 %collective-permute-start.155 = (bf16[2,1024,1024]{2,1,0:T(8,128)(2,1)}, bf16[2,1024,1024]{2,1,0:T(8,128)(2,1)}, u32[]{:S(2)}, u32[]{:S(2)}) collective-permute-start(bf16[2,1024,1024]{2,1,0:T(8,128)(2,1)} %pad_maximum_fusion), channel_id=1, source_target_pairs={{0,16},{16,0},{1,17},{17,1},{2,18},{18,2},{3,19},{19,3},{4,20},{20... | collective-permute-start | bytes 12582920 | tf_op jit(solution)/shard_map/ppermute | solution.py:23
  1202.8 70.7 %reduce-scatter.35.cloned.1.call-start = ((), (), s32[]{:S(2)}) async-start(), calls=%async_computation.25 | async-start | bytes 983040 | tf_op jit(solution)/shard_map/reduce_scatter | solution.py:615
  (489 other events, 5846.8 us)
Sparse Core Ops, SparseCore 0:
  69.6 103.3 all-gather.8
  174.6 30.0 all-gather.10
  287.4 108.0 all-gather.12
  411.6 28.3 all-gather.14
  614.0 80.3 reduce-scatter.12
  720.2 52.8 reduce-scatter.14
  776.4 26.0 reduce-scatter.16
  804.9 25.7 reduce-scatter.18
  844.1 17.3 reduce-scatter.20
  916.1 31.2 reduce-scatter.22
  1000.4 64.2 reduce-scatter.24
  1070.7 53.0 reduce-scatter.26
  1142.2 26.0 reduce-scatter.28
  1171.0 25.7 reduce-scatter.30
  1203.0 18.1 reduce-scatter.32
  1251.7 21.7 reduce-scatter.34

commit v2 on v1

--- a/solution.py
+++ b/solution.py
@@ -33,6 +33,10 @@
 
 def after(value, earlier):
     return lax.optimization_barrier((value, earlier))[0]
+
+
+def unchanged(value):
+    return value
 
 
 def low(value):
@@ -157,6 +161,10 @@
     @pl.when(pl.program_id(0) == pl.num_programs(0) - 1)
     def _():
         store_parts(total, parts)
+
+
+def in_hbm(arrays):
+    return [pltpu.with_memory_space_constraint(arr, pltpu.HBM) for arr in arrays]
 
 
 def mlp_call(kernel, blocks, streamed, resident, hidden_outs, weights):
@@ -192,8 +200,8 @@
         + [columns for _ in streamed]
         + weight_specs
         + [whole(arr.shape) for arr in resident],
-        out_shape=[jax.ShapeDtypeStruct((rows, hidden), jnp.bfloat16)] * hidden_outs
-        + [jax.ShapeDtypeStruct((rows, width), jnp.bfloat16)]
+        out_shape=[pltpu.HBM((rows, hidden), jnp.bfloat16)] * hidden_outs
+        + [pltpu.HBM((rows, width), jnp.bfloat16)]
         + [jax.ShapeDtypeStruct((size, width), kind) for kind in part_types],
         out_specs=[columns] * hidden_outs
         + [whole((rows, width))]
@@ -205,7 +213,7 @@
             bytes_accessed=4 * width * hidden + 6 * rows * width,
             transcendentals=2 * rows * hidden,
         ),
-    )(*blocks, *streamed, *matrices, *resident)
+    )(*blocks, *in_hbm(streamed), *in_hbm(matrices), *in_hbm(resident))
     return outs[:hidden_outs], outs[hidden_outs], outs[hidden_outs + 1 :]
 
 
@@ -520,22 +528,25 @@
     return 0 if is_square("wide") else lax.axis_index("wide") * size
 
 
-def dense_forward(block_in, segment_ids, weights, order, change):
+def dense_forward(block_in, segment_ids, weights, order, change_after, hooks):
+    early_hook, middle_hook, late_hook = hooks
     first_norm_gain, qkv_mat, out_mat, second_norm_gain, mlp_weights = weights
     own_size = block_in.shape[0]
     shaped_one, normal_one, inv_one = norm_forward(block_in, first_norm_gain)
-    first_blocks = wide_spread(low(shaped_one))
+    first_blocks = wide_spread(early_hook(low(shaped_one)))
     packed = order.to_tokens(joined([low(matmul(rows, qkv_mat)) for rows in first_blocks]))
     attended, log_totals = attention_forward(packed, segment_ids)
+    change = change_after(attended)
     attended = order.from_tokens(attended)
     middle = block_in + wide_collect([matmul(rows, out_mat) for rows in split(attended)])
     shaped_two, normal_two, inv_two = norm_forward(middle, second_norm_gain)
-    second_blocks = wide_spread(low(shaped_two))
+    second_blocks = middle_hook(wide_spread(low(shaped_two)))
     rows = jnp.arange(change.shape[0], dtype=jnp.int32)
     moving = (change[:, None] == rows[None, :]).astype(jnp.bfloat16)
     own_rows = own_start(own_size) + jnp.arange(own_size, dtype=jnp.int32)
     own_moving = (change[:, None] == own_rows[None, :]).astype(jnp.bfloat16)
     parts, mlp_saved = mlp_forward(second_blocks, mlp_weights, (moving, own_moving, low(middle)))
+    parts = late_hook(parts)
     return (
         wide_collect(parts),
         (
@@ -573,26 +584,27 @@
     parts, grad_wide, grad_pre = mlp_backward(blocks, slope, mlp_weights, (moving,))
     grad_out = lax.dynamic_slice_in_dim(grad_wide, own_start(own_size), own_size, 0)
     grad_norm_two = wide_collect(parts)
-    down_part = half_summed(weight_grad([activated], [grad_wide]), 0)
-    up_part = half_summed(weight_grad([second_rows], [grad_pre]), 1)
+    down_part = half_given(weight_grad([activated], [grad_wide]), 0)
+    up_part = half_given(weight_grad([second_rows], [grad_pre]), 1)
     grad_norm_two, down_part, up_part = together((grad_norm_two, down_part, up_part))
-    grad_down, grad_up = rep_summed(down_part, 1), rep_summed(up_part, 0)
     grad_in_two, grad_gain_two = norm_backward(grad_norm_two, normal_two, inv_two, second_norm_gain)
     grad_middle = grad_out.astype(jnp.float32) + grad_in_two
-    mid_blocks, last_sum = together((wide_spread(low(grad_middle)), last_sum))
+    down_part, up_part = half_sum(down_part, 0), half_sum(up_part, 1)
+    mid_blocks, last_sum, down_part, up_part = together(
+        (wide_spread(low(grad_middle)), last_sum, down_part, up_part)
+    )
+    grad_down, grad_up = rep_summed(down_part, 1), rep_summed(up_part, 0)
     finished = finish([last_sum, sums])
     grad_att = order.to_tokens(joined([low(matmul_right(rows, out_mat)) for rows in mid_blocks]))
     grad_packed = attention_backward(packed, segment_ids, log_totals, grad_att)
-    out_part = half_summed(low(matmul_left(attended, joined(mid_blocks))), 0)
-    grad_packed, out_part, grad_down, grad_up = together(
-        (grad_packed, out_part, grad_down, grad_up)
-    )
+    out_part = half_summed(weight_grad(row_blocks(attended, len(mid_blocks)), mid_blocks), 0)
+    grad_packed, out_part = together((grad_packed, out_part))
     grad_packed = order.from_tokens(grad_packed)
     grad_norm_one = wide_collect([matmul_right(rows, qkv_mat) for rows in split(grad_packed)])
-    qkv_part = half_summed(low(matmul_left(joined(first_blocks), grad_packed)), 1)
+    qkv_part = half_summed(weight_grad(first_blocks, row_blocks(grad_packed, len(first_blocks))), 1)
     grad_out_mat = rep_summed(out_part, 1)
-    grad_norm_one, qkv_part, finished, grad_out_mat = together(
-        (grad_norm_one, qkv_part, finished, grad_out_mat)
+    grad_norm_one, qkv_part, finished, grad_down, grad_up = together(
+        (grad_norm_one, qkv_part, finished, grad_down, grad_up)
     )
     grad_qkv = rep_summed(qkv_part, 0)
     grad_in_one, grad_gain_one = norm_backward(grad_norm_one, normal_one, inv_one, first_norm_gain)
@@ -603,12 +615,22 @@
     )
 
 
+def half_given(partial, dim):
+    size = partial.shape[dim] // 2
+    other = (1 - lax.axis_index("section")) * size
+    return partial, section_swap(lax.dynamic_slice_in_dim(partial, other, size, dim))
+
+
+def half_sum(given, dim):
+    partial, moved = given
+    size = partial.shape[dim] // 2
+    own = lax.axis_index("section") * size
+    kept = lax.dynamic_slice_in_dim(partial, own, size, dim)
+    return low(kept.astype(jnp.float32) + moved.astype(jnp.float32))
+
+
 def half_summed(partial, dim):
-    section = lax.axis_index("section")
-    size = partial.shape[dim] // 2
-    kept = lax.dynamic_slice_in_dim(partial, section * size, size, dim)
-    given = lax.dynamic_slice_in_dim(partial, (1 - section) * size, size, dim)
-    return low(kept.astype(jnp.float32) + section_swap(given).astype(jnp.float32))
+    return half_sum(half_given(partial, dim), dim)
 
 
 def rep_summed(partial, dim):
@@ -645,20 +667,29 @@
     out[...] = low(total)
 
 
-def weight_grad(rows, grads, rows_half=None, columns_half=None):
-    height, width = rows[0].shape[1], grads[0].shape[1]
-    if rows_half is not None:
-        height = height // 2
-    if columns_half is not None:
-        width = width // 2
+def row_blocks(values, count):
+    return [(values, i, count) for i in range(count)]
+
+
+def weight_grad(rows, grads):
+    rows, grads = [
+        [item if isinstance(item, tuple) else (item, 0, 1) for item in items] for items in (rows, grads)
+    ]
+    height, width = rows[0][0].shape[1], grads[0][0].shape[1]
     tile = hidden_tile(height)
-    first, column = (rows_half or 0) * (height // tile), columns_half or 0
-    depth = sum(arr.shape[0] for arr in rows)
+
+    def block(item, columns, moving):
+        arr, number, count = item
+        return pl.BlockSpec(
+            (arr.shape[0] // count, columns), lambda i: (number, i if moving else 0)
+        )
+
+    depth = sum(arr.shape[0] // count for arr, _, count in rows)
     return pl.pallas_call(
         functools.partial(weight_grad_kernel, len(rows)),
         grid=(height // tile,),
-        in_specs=[pl.BlockSpec((arr.shape[0], tile), lambda i: (0, i + first)) for arr in rows]
-        + [pl.BlockSpec((arr.shape[0], width), lambda i: (0, column)) for arr in grads],
+        in_specs=[block(item, tile, True) for item in rows]
+        + [block(item, width, False) for item in grads],
         out_shape=jax.ShapeDtypeStruct((height, width), jnp.bfloat16),
         out_specs=pl.BlockSpec((tile, width), lambda i: (i, 0)),
         compiler_params=pltpu.CompilerParams(vmem_limit_bytes=24 * 2**20),
@@ -667,7 +698,7 @@
             bytes_accessed=2 * (depth * (height + width) + height * width),
             transcendentals=0,
         ),
-    )(*rows, *grads)
+    )(*[item[0] for item in rows], *[item[0] for item in grads])
 
 
 def chunked(values):
@@ -816,7 +847,13 @@
             bytes_accessed=8 * width * width + 16 * depth * width,
             transcendentals=0,
         ),
-    )(lax.axis_index("section").reshape(1), *rows, *grads_pre, *acts, *grads_wide)
+    )(
+        lax.axis_index("section").reshape(1),
+        *in_hbm(rows),
+        *in_hbm(grads_pre),
+        *in_hbm(acts),
+        *in_hbm(grads_wide),
+    )
     return low(kept.astype(jnp.float32) + section_swap(given).astype(jnp.float32))
 
 
@@ -898,9 +935,14 @@
         [jnp.where(is_first, own_routes, other_routes), jnp.where(is_first, other_routes, own_routes)]
     )
     route_tables = wide_table(layer_routes)
-    plane_rows = route_table.shape[1] * lax.axis_size("wide")
-    orders = [token_order(plane_rows)] + [routed_order(route_tables[:, i]) for i in range(2)]
-    changes = [order_change(orders[i], orders[i + 1]) for i in range(2)]
+    orders = [token_order(route_table.shape[1] * lax.axis_size("wide")), None, None]
+
+    def change_after(layer):
+        def change(event):
+            orders[layer + 1] = routed_order(after(route_tables[:, layer], event))
+            return order_change(orders[layer], orders[layer + 1])
+
+        return change
 
     def stacked_layers(own):
         return lax.all_gather(own, "section", axis=0, tiled=True)
@@ -914,12 +956,11 @@
             piece = jnp.where(is_first, expert_ups, section_send(expert_downs, 0))
         else:
             piece = jnp.where(is_first, section_send(expert_ups, 1), expert_downs)
-        return rep_pair_gather(piece[None])
+        return piece[None]
 
     segment_ids = mine(segments)
     hidden = mine(tokens_in)
     expert_ups, expert_downs = after((expert_up[0, 0], expert_down[0, 0]), hidden)
-    gathered = split_layer(0)
     layer_matrices = [None, None]
     second_inputs = (expert_ups, expert_downs)
 
@@ -946,17 +987,30 @@
     grad = expert_trade(low(matmul_left(slot_matrix, mine(cotangent))))
     saved = []
     for layer in range(2):
+        gathering = []
+
+        def early(value):
+            value, piece = together((value, split_layer(0)))
+            gathering.append(rep_pair_gather(piece))
+            return value
+
+        def later(value):
+            value, own_gathered = together((value, gathering[0] if layer == 0 else gathered))
+            gathering.append(own_gathered)
+            return value
+
         rows_in, dense_saved = dense_forward(
             hidden.astype(jnp.float32),
             segment_ids,
             dense_weights[layer],
             orders[layer],
-            changes[layer],
+            change_after(layer),
+            (early, unchanged, later) if layer == 0 else (unchanged, later, unchanged),
         )
-        layer_matrices[layer] = stacked_layers(after(gathered, dense_saved[-2][0])[None])
+        layer_matrices[layer] = stacked_layers(gathering[-1][None])
         if layer == 0:
             expert_ups, expert_downs = after(second_inputs, rows_in)
-            gathered = split_layer(1)
+            gathered = rep_pair_gather(split_layer(1))
         hidden, expert_saved = expert_forward(rows_in, *expert_weights(layer))
         saved.append((dense_saved, expert_saved))
     produced = low(matmul(slot_matrix, expert_trade(hidden)))

time: 1300 us -> 1260 us (0.969)
  Pallas kernels: 212 us -> 254 us
  local copies, waits for them, and re-layouts: 87.4 us -> 47.2 us
  other arithmetic: 167 us -> 141 us
  waiting for transfers between devices: 536 us -> 553 us
  matrix products: 83.8 us -> 67.5 us
    unnamed x660 -> x482, local copies, waits for them, and re-layouts: 66.5 us -> 32.4 us
    pallas_call x20, Pallas kernels: 159 us -> 185 us  [mlp_call(): pl.pallas_call(functools.partial(kernel, count, len(resident) > 0, len(we...]
    ppermute x32, waiting for transfers between devices: 297 us -> 319 us  [rep_hop(): return lax.ppermute(value, 'rep', [(i, i ^ mask) for i in range(4)])]
    all_gather x2, waiting for transfers between devices: 28.3 us -> 10 us  [rep_pair_gather(): lax.all_gather(values, 'rep', axis=0, tiled=True, axis_index_groups=rep_p...]
    reduce_scatter x8, waiting for transfers between devices: 6.52 us -> 19.6 us  [rep_summed(): return lax.psum_scatter(partial, 'rep', scatter_dimension=dim, tiled=True)]
    convert_element_type x35 -> x37, other arithmetic: 51.7 us -> 45.1 us  [low(): return value.astype(jnp.bfloat16)]
  transfers between devices with their start and end apart: 191 -> 191, of which waited for: 92 -> 97; matrix products, arithmetic and copies ran while one was open for 20% -> 17% of each run, Pallas kernels for 14% -> 17%
where the time goes in v2:
time: 1260 us; the launch traced here: 1250 us
  waiting for transfers between devices  553 us (44%)
  Pallas kernels  254 us (20%)
  starting transfers between devices  172 us (14%)
  other arithmetic  141 us (11%)
  matrix products  67.5 us (5%)
  local copies, waits for them, and re-layouts  47.2 us (4%)
  between operations  19 us (2%)
    ppermute x32, waiting for transfers between devices, rep_hop(): return lax.ppermute(value, 'rep', [(i, i ^ mask) for i in range(4)])  319 us
    ppermute x99, waiting for transfers between devices, wide_hop(): return lax.ppermute(value, 'wide', [(i, i ^ mask) for i in range(4)])  190 us
    pallas_call x20, Pallas kernels, mlp_call(): pl.pallas_call(functools.partial(kernel, count, len(resident) > 0, len(we...  185 us
    ppermute x99, starting transfers between devices, wide_hop(): return lax.ppermute(value, 'wide', [(i, i ^ mask) for i in range(4)])  104 us
    convert_element_type x37, other arithmetic, low(): return value.astype(jnp.bfloat16)  45.1 us
    pallas_call x4, Pallas kernels, pair_weight_grads(): pl.pallas_call(functools.partial(pair_weight_kernel, count), out_shape=[j...  42.7 us
    ppermute x32, starting transfers between devices, rep_hop(): return lax.ppermute(value, 'rep', [(i, i ^ mask) for i in range(4)])  34.7 us
    unnamed x482, local copies, waits for them, and re-layouts  32.4 us
  transfers between devices with their start and end apart: 191, of which 97 were waited for; matrix products, arithmetic and copies ran while one was open for 17% of the time, Pallas kernels for 17%

profile of v2, /device:TPU:0, one launch (start us, length us, event | category | flops | bytes accessed | tf_op | source)
XLA Modules:
  0.0 1254.2 jit_solution(15674449298809018274)
XLA Ops:
  125.4 14.5 %shard_map.229 = (bf16[1024,1024]{1,0:T(8,128)(2,1)}, bf16[1024,1024]{1,0:T(8,128)(2,1)}, bf16[1024,1024]{1,0:T(8,128)(2,1)}, f32[256,1024]{1,0:T(8,128)S(1)}, b...) custom-call(bf16[256,1024]{1,0:T(8,128)(2,1)S(1)} %multiply_convert_fusion.5.refs_0_, ...), custom_call_target="tpu_custom_call" | custom-call | flops 4294967296 | bytes 10485760 | tf_op jit(solution)/shard_map/pallas_call | solution.py:196
  179.8 15.1 %collective-permute-done.41.refs_1_ = bf16[128,1024]{1,0:T(8,128)(2,1)S(1)} collective-permute-done((bf16[128,1024]{1,0:T(8,128)(2,1)S(1)}, bf16[128,1024]{1,0:T(8,128)(2,1)S(1)}, u32[]{:S(2)}, u32[]{:S(2)}) %collective-permute-start.41) | collective-permute-done | bytes 262176 | tf_op jit(solution)/shard_map/ppermute | solution.py:315
  236.0 12.1 collective-permute-done.43.refs_1_
  367.5 16.4 %shard_map.234 = (bf16[1024,1024]{1,0:T(8,128)(2,1)}, bf16[1024,1024]{1,0:T(8,128)(2,1)}, bf16[1024,1024]{1,0:T(8,128)(2,1)}, f32[256,1024]{1,0:T(8,128)S(1)}, b...) custom-call(bf16[256,1024]{1,0:T(8,128)(2,1)S(1)} %multiply_convert_fusion.4.refs_0_, ...), custom_call_target="tpu_custom_call" | custom-call | flops 4294967296 | bytes 10485760 | tf_op jit(solution)/shard_map/pallas_call | solution.py:196
  414.5 12.5 collective-permute-done.67.refs_1_
  446.9 12.0 collective-permute-done.68
  459.6 16.2 %collective-permute-done.75 = bf16[128,1024]{1,0:T(8,128)(2,1)S(1)} collective-permute-done((bf16[128,1024]{1,0:T(8,128)(2,1)S(1)}, bf16[128,1024]{1,0:T(8,128)(2,1)S(1)}, u32[]{:S(2)}, u32[]{:S(2)}) %collective-permute-start.75) | collective-permute-done | bytes 262176 | tf_op jit(solution)/shard_map/ppermute | solution.py:315
  520.0 17.3 %collective-permute-done.76.refs_1_ = bf16[128,1024]{1,0:T(8,128)(2,1)S(1)} collective-permute-done((bf16[128,1024]{1,0:T(8,128)(2,1)S(1)}, bf16[128,1024]{1,0:T(8,128)(2,1)S(1)}, u32[]{:S(2)}, u32[]{:S(2)}) %collective-permute-start.76) | collective-permute-done | bytes 262176 | tf_op jit(solution)/shard_map/ppermute | solution.py:315
  553.2 10.4 shard_map.242
  563.8 13.7 %collective-permute-done.81.refs_1_ = bf16[128,1024]{1,0:T(8,128)(2,1)S(1)} collective-permute-done((bf16[128,1024]{1,0:T(8,128)(2,1)S(1)}, bf16[128,1024]{1,0:T(8,128)(2,1)S(1)}, u32[]{:S(2)}, u32[]{:S(2)}) %collective-permute-start.81) | collective-permute-done | bytes 262176 | tf_op jit(solution)/shard_map/ppermute | solution.py:315
  585.2 14.8 %collective-permute-done.82 = bf16[128,1024]{1,0:T(8,128)(2,1)S(1)} collective-permute-done((bf16[128,1024]{1,0:T(8,128)(2,1)S(1)}, bf16[128,1024]{1,0:T(8,128)(2,1)S(1)}, u32[]{:S(2)}, u32[]{:S(2)}) %collective-permute-start.82) | collective-permute-done | bytes 262176 | tf_op jit(solution)/shard_map/ppermute | solution.py:315
  608.1 16.2 %collective-permute-done.77 = bf16[128,1024]{1,0:T(8,128)(2,1)S(1)} collective-permute-done((bf16[128,1024]{1,0:T(8,128)(2,1)S(1)}, bf16[128,1024]{1,0:T(8,128)(2,1)S(1)}, u32[]{:S(2)}, u32[]{:S(2)}) %collective-permute-start.77) | collective-permute-done | bytes 262176 | tf_op jit(solution)/shard_map/ppermute | solution.py:315
  631.9 14.4 %collective-permute-done.86.refs_1_ = bf16[128,1024]{1,0:T(8,128)(2,1)S(1)} collective-permute-done((bf16[128,1024]{1,0:T(8,128)(2,1)S(1)}, bf16[128,1024]{1,0:T(8,128)(2,1)S(1)}, u32[]{:S(2)}, u32[]{:S(2)}) %collective-permute-start.86) | collective-permute-done | bytes 262176 | tf_op jit(solution)/shard_map/ppermute | solution.py:315
  666.6 13.3 %collective-permute-done.87 = bf16[128,1024]{1,0:T(8,128)(2,1)S(1)} collective-permute-done((bf16[128,1024]{1,0:T(8,128)(2,1)S(1)}, bf16[128,1024]{1,0:T(8,128)(2,1)S(1)}, u32[]{:S(2)}, u32[]{:S(2)}) %collective-permute-start.87) | collective-permute-done | bytes 262176 | tf_op jit(solution)/shard_map/ppermute | solution.py:315
  707.1 13.2 %shard_map.245 = (bf16[1024,1024]{1,0:T(8,128)(2,1)}, bf16[1024,1024]{1,0:T(8,128)(2,1)}, f32[256,1024]{1,0:T(8,128)S(1)}, bf16[256,1024]{1,0:T(8,128)(2,1)S(1)}...) custom-call(bf16[256,1024]{1,0:T(8,128)(2,1)S(1)} %pad_maximum_fusion.19.refs_0_, ...), custom_call_target="tpu_custom_call" | custom-call | flops 4294967296 | bytes 10485760 | tf_op jit(solution)/shard_map/pallas_call | solution.py:196
  835.1 16.3 %collective-permute-done.121.refs_1_ = bf16[128,1024]{1,0:T(8,128)(2,1)S(1)} collective-permute-done((bf16[128,1024]{1,0:T(8,128)(2,1)S(1)}, bf16[128,1024]{1,0:T(8,128)(2,1)S(1)}, u32[]{:S(2)}, u32[]{:S(2)}) %collective-permute-start.121) | collective-permute-done | bytes 262176 | tf_op jit(solution)/shard_map/ppermute | solution.py:315
  866.8 11.7 shard_map.253
  883.9 22.6 %collective-permute-done.123 = bf16[128,1024]{1,0:T(8,128)(2,1)} collective-permute-done((bf16[128,1024]{1,0:T(8,128)(2,1)S(1)}, bf16[128,1024]{1,0:T(8,128)(2,1)}, u32[]{:S(2)}, u32[]{:S(2)}) %collective-permute-start.123) | collective-permute-done | bytes 262176 | tf_op jit(solution)/shard_map/ppermute | solution.py:315
  916.6 25.2 %collective-permute-done.119.refs_1_ = bf16[128,1024]{1,0:T(8,128)(2,1)S(1)} collective-permute-done((bf16[128,1024]{1,0:T(8,128)(2,1)S(1)}, bf16[128,1024]{1,0:T(8,128)(2,1)S(1)}, u32[]{:S(2)}, u32[]{:S(2)}) %collective-permute-start.119) | collective-permute-done | bytes 262176 | tf_op jit(solution)/shard_map/ppermute | solution.py:315
  949.6 14.3 %collective-permute-done.120 = bf16[128,1024]{1,0:T(8,128)(2,1)S(1)} collective-permute-done((bf16[128,1024]{1,0:T(8,128)(2,1)S(1)}, bf16[128,1024]{1,0:T(8,128)(2,1)S(1)}, u32[]{:S(2)}, u32[]{:S(2)}) %collective-permute-start.120) | collective-permute-done | bytes 262176 | tf_op jit(solution)/shard_map/ppermute | solution.py:315
  970.5 13.7 %collective-permute-done.124.refs_1_ = bf16[128,1024]{1,0:T(8,128)(2,1)S(1)} collective-permute-done((bf16[128,1024]{1,0:T(8,128)(2,1)S(1)}, bf16[128,1024]{1,0:T(8,128)(2,1)S(1)}, u32[]{:S(2)}, u32[]{:S(2)}) %collective-permute-start.124) | collective-permute-done | bytes 262176 | tf_op jit(solution)/shard_map/ppermute | solution.py:315
  991.9 10.4 shard_map.255
  1002.8 14.7 %collective-permute-done.125 = bf16[128,1024]{1,0:T(8,128)(2,1)S(1)} collective-permute-done((bf16[128,1024]{1,0:T(8,128)(2,1)S(1)}, bf16[128,1024]{1,0:T(8,128)(2,1)S(1)}, u32[]{:S(2)}, u32[]{:S(2)}) %collective-permute-start.125) | collective-permute-done | bytes 262176 | tf_op jit(solution)/shard_map/ppermute | solution.py:315
  1055.9 13.3 %shard_map.256 = (bf16[1024,1024]{1,0:T(8,128)(2,1)}, bf16[1024,1024]{1,0:T(8,128)(2,1)}, f32[256,1024]{1,0:T(8,128)S(1)}, bf16[256,1024]{1,0:T(8,128)(2,1)S(1)}...) custom-call(bf16[256,1024]{1,0:T(8,128)(2,1)S(1)} %pad_maximum_fusion.26.refs_0_, ...), custom_call_target="tpu_custom_call" | custom-call | flops 4294967296 | bytes 10485760 | tf_op jit(solution)/shard_map/pallas_call | solution.py:196
  (1275 shorter events, 881.0 us)
Async XLA Ops:
  7.2 143.4 %all-gather.8.cloned.1.call-start = ((), (), s32[]{:S(2)}) async-start(), calls=%async_computation.14 | async-start | bytes 12582912 | tf_op jit(solution)/shard_map/all_gather | solution.py:322
  32.7 74.4 %collective-permute-start.25 = (bf16[1024,1024]{1,0:T(8,128)(2,1)}, bf16[1024,1024]{1,0:T(8,128)(2,1)}, u32[]{:S(2)}, u32[]{:S(2)}) collective-permute-start(bf16[1024,1024]{1,0:T(8,128)(2,1)} %bitcast.566), channel_id=1, source_target_pairs={{0,16},{16,0},{1,17},{17,1},{2,18},{18,2},{3,19},{19,3},{4,20},{20... | collective-permute-start | bytes 6291464 | tf_op jit(solution)/shard_map/ppermute | solution.py:23
  46.4 148.5 %all-gather.10.cloned.1.call-start = ((), (), s32[]{:S(2)}) async-start(), calls=%async_computation.27 | async-start | bytes 25165824 | tf_op jit(solution)/shard_map/all_gather | solution.py:948
  150.7 209.4 %all-gather.12.cloned.1.call-start = ((), (), s32[]{:S(2)}) async-start(), calls=%async_computation.28 | async-start | bytes 12582912 | tf_op jit(solution)/shard_map/all_gather | solution.py:322
  154.8 73.3 %collective-permute-start.63 = (bf16[2,1024,1024]{2,1,0:T(8,128)(2,1)}, bf16[2,1024,1024]{2,1,0:T(8,128)(2,1)}, u32[]{:S(2)}, u32[]{:S(2)}) collective-permute-start(bf16[2,1024,1024]{2,1,0:T(8,128)(2,1)} %bitcast.531), channel_id=1, source_target_pairs={{16,0},{17,1},{18,2},{19,3},{20,4},{21,5},{22,6},{23,7},{24,8},{25... | collective-permute-start | bytes 12582920 | tf_op jit(solution)/shard_map/ppermute | solution.py:27
  232.8 194.2 %all-gather.14.cloned.1.call-start = ((), (), s32[]{:S(2)}) async-start(), calls=%async_computation.29 | async-start | bytes 25165824 | tf_op jit(solution)/shard_map/all_gather | solution.py:948
  392.7 314.3 %reduce-scatter.13.cloned.1.call-start = ((), (), s32[]{:S(2)}) async-start(), calls=%async_computation.15 | async-start | bytes 6291456 | tf_op jit(solution)/shard_map/reduce_scatter | solution.py:326
  435.8 53.7 %collective-permute-start.79 = (bf16[128,1024]{1,0:T(8,128)(2,1)S(1)}, bf16[128,1024]{1,0:T(8,128)(2,1)S(1)}, u32[]{:S(2)}, u32[]{:S(2)}) collective-permute-start(bf16[128,1024]{1,0:T(8,128)(2,1)S(1)} %fusion.182.refs_0_), channel_id=1, source_target_pairs={{0,2},{1,3},{2,0},{3,1},{4,6},{5,7},{6,4},{7,5},{8,10},{9,11},{10,... | collective-permute-start | bytes 786440 | tf_op jit(solution)/shard_map/ppermute | solution.py:315
  563.6 37.2 %collective-permute-start.84 = (bf16[2,1024,1024]{2,1,0:T(8,128)(2,1)S(1)}, bf16[2,1024,1024]{2,1,0:T(8,128)(2,1)S(1)}, u32[]{:S(2)}, u32[]{:S(2)}) collective-permute-start(bf16[2,1024,1024]{2,1,0:T(8,128)(2,1)S(1)} %get-tuple-element.336), channel_id=1, source_target_pairs={{0,16},{16,0},{1,17},{17,1},{2,18},{18,2},{3,19},{19,3},{4,20},{20... | collective-permute-start | bytes 12582920 | tf_op jit(solution)/shard_map/ppermute | solution.py:23
  605.1 168.1 %reduce-scatter.15.cloned.1.call-start = ((), (), s32[]{:S(2)}) async-start(), calls=%async_computation.16 | async-start | bytes 6291456 | tf_op jit(solution)/shard_map/reduce_scatter | solution.py:326
  664.5 38.2 %collective-permute-start.94 = (bf16[2,1024,1024]{2,1,0:T(8,128)(2,1)S(1)}, bf16[2,1024,1024]{2,1,0:T(8,128)(2,1)S(1)}, u32[]{:S(2)}, u32[]{:S(2)}) collective-permute-start(bf16[2,1024,1024]{2,1,0:T(8,128)(2,1)S(1)} %get-tuple-element.353), channel_id=1, source_target_pairs={{0,16},{16,0},{1,17},{17,1},{2,18},{18,2},{3,19},{19,3},{4,20},{20... | collective-permute-start | bytes 12582920 | tf_op jit(solution)/shard_map/ppermute | solution.py:23
  707.0 117.2 %reduce-scatter.17.cloned.1.call-start = ((), (), s32[]{:S(2)}) async-start(), calls=%async_computation.17 | async-start | bytes 1310720 | tf_op jit(solution)/shard_map/reduce_scatter | solution.py:637
  776.0 54.4 %reduce-scatter.19.cloned.1.call-start = ((), (), s32[]{:S(2)}) async-start(), calls=%async_computation.18 | async-start | bytes 1310720 | tf_op jit(solution)/shard_map/reduce_scatter | solution.py:637
  793.6 176.7 %reduce-scatter.23.cloned.1.call-start = ((), (), s32[]{:S(2)}) async-start(), calls=%async_computation.20 | async-start | bytes 327680 | tf_op jit(solution)/shard_map/reduce_scatter | solution.py:637
  880.5 83.4 %collective-permute-start.122 = (bf16[2,1024,1024]{2,1,0:T(8,128)(2,1)}, bf16[2,1024,1024]{2,1,0:T(8,128)(2,1)}, u32[]{:S(2)}, u32[]{:S(2)}) collective-permute-start(bf16[2,1024,1024]{2,1,0:T(8,128)(2,1)} %get-tuple-element.399), channel_id=1, source_target_pairs={{0,16},{16,0},{1,17},{17,1},{2,18},{18,2},{3,19},{19,3},{4,20},{20... | collective-permute-start | bytes 12582920 | tf_op jit(solution)/shard_map/ppermute | solution.py:23
  880.6 89.8 %reduce-scatter.21.cloned.1.call-start = ((), (), s32[]{:S(2)}) async-start(), calls=%async_computation.19 | async-start | bytes 983040 | tf_op jit(solution)/shard_map/reduce_scatter | solution.py:637
  883.8 159.4 %reduce-scatter.25.cloned.1.call-start = ((), (), s32[]{:S(2)}) async-start(), calls=%async_computation.21 | async-start | bytes 6291456 | tf_op jit(solution)/shard_map/reduce_scatter | solution.py:326
  970.4 153.6 %reduce-scatter.27.cloned.1.call-start = ((), (), s32[]{:S(2)}) async-start(), calls=%async_computation.22 | async-start | bytes 6291456 | tf_op jit(solution)/shard_map/reduce_scatter | solution.py:326
  1048.6 141.7 %reduce-scatter.35.cloned.1.call-start = ((), (), s32[]{:S(2)}) async-start(), calls=%async_computation.26 | async-start | bytes 327680 | tf_op jit(solution)/shard_map/reduce_scatter | solution.py:637
  1093.1 52.8 %collective-permute-start.78 = (bf16[256,512]{1,0:T(8,128)(2,1)}, bf16[256,512]{1,0:T(8,128)(2,1)}, u32[]{:S(2)}, u32[]{:S(2)}) collective-permute-start(bf16[256,512]{1,0:T(8,128)(2,1)} %constant_dynamic-slice_fusion.21), channel_id=1, source_target_pairs={{0,16},{16,0},{1,17},{17,1},{2,18},{18,2},{3,19},{19,3},{4,20},{20... | collective-permute-start | bytes 786440 | tf_op jit(solution)/shard_map/ppermute | solution.py:23
  1144.3 66.2 %reduce-scatter.29.cloned.1.call-start = ((), (), s32[]{:S(2)}) async-start(), calls=%async_computation.23 | async-start | bytes 1310720 | tf_op jit(solution)/shard_map/reduce_scatter | solution.py:637
  1147.0 72.4 %reduce-scatter.31.cloned.1.call-start = ((), (), s32[]{:S(2)}) async-start(), calls=%async_computation.24 | async-start | bytes 1310720 | tf_op jit(solution)/shard_map/reduce_scatter | solution.py:637
  1159.3 37.2 %collective-permute-start.155 = (bf16[2,1024,1024]{2,1,0:T(8,128)(2,1)}, bf16[2,1024,1024]{2,1,0:T(8,128)(2,1)}, u32[]{:S(2)}, u32[]{:S(2)}) collective-permute-start(bf16[2,1024,1024]{2,1,0:T(8,128)(2,1)} %pad_maximum_fusion), channel_id=1, source_target_pairs={{0,16},{16,0},{1,17},{17,1},{2,18},{18,2},{3,19},{19,3},{4,20},{20... | collective-permute-start | bytes 12582920 | tf_op jit(solution)/shard_map/ppermute | solution.py:23
  1160.7 83.4 %reduce-scatter.33.cloned.1.call-start = ((), (), s32[]{:S(2)}) async-start(), calls=%async_computation.25 | async-start | bytes 983040 | tf_op jit(solution)/shard_map/reduce_scatter | solution.py:637
  (404 other events, 6872.0 us)
Sparse Core Ops, SparseCore 0:
  46.5 104.1 all-gather.7
  152.2 30.0 all-gather.9
  232.9 121.9 all-gather.11
  360.2 29.1 all-gather.13
  605.2 70.6 reduce-scatter.12
  707.1 52.1 reduce-scatter.14
  776.1 26.0 reduce-scatter.16
  804.7 25.7 reduce-scatter.18
  880.7 32.2 reduce-scatter.22
  915.8 26.5 reduce-scatter.20
  970.5 64.4 reduce-scatter.24
  1043.4 52.9 reduce-scatter.26
  1144.4 18.7 reduce-scatter.34
  1165.4 25.2 reduce-scatter.28
  1193.5 25.8 reduce-scatter.30
  1222.1 21.9 reduce-scatter.32
